TPU v7x, 32 devices: a whole 2x2x4 slice. The times are simulated.
32 devices in a mesh: ctx: 8 (over z, y), head: 4 (over x, core).
Axes of the slice: x: 2, y: 2, z: 4, core: 2. Of those that a mesh axis runs over, the one named last changes fastest.
Arguments:
- conv_input: bfloat16 [6144, 8448], P(('ctx', 'head')), may hold values from -6 to 6
- conv_weight: float32 [4, 8448], replicated, may hold values from -3 to 3
- conv_bias: float32 [8448], replicated, may hold values from -3 to 3
- step_size: float32 [128, 6144], P('head', 'ctx'), may hold values from 0 to 0.12, as said below
- log_decay: float32 [128, 6144], P('head', 'ctx'), may hold values from -0.6 to 0, as said below
- skip_gain: float32 [128], P('head'), may hold values from 0.5 to 2
- grad_output: bfloat16 [6144, 8192], P('ctx', 'head'), may hold values from -6 to 6
Outputs:
- layer_output: bfloat16 [6144, 8192], P('ctx', 'head')
- grad_input: bfloat16 [6144, 8448], P(('ctx', 'head'))
- grad_step: float32 [128, 6144], P('head', 'ctx')
- grad_decay: float32 [128, 6144], P('head', 'ctx')
Inputs may be any that keep to these rules, and one draw needn't show every extreme that they name: `step_size`: positive step sizes. `log_decay`: negative logarithms of decays.
All inputs are finite; a program needn't handle non-finite values.
Results may differ from a plain program's by a relative error of at most 0.013.
Values may be sent and summed in bfloat16 or wider, within the bound.
A program may use at most 128 MiB of HBM per device.

v0:
```python
from functools import partial

import jax
import jax.numpy as jnp
from jax import lax
from jax.sharding import PartitionSpec as P

STATE = 128
BLOCK = 256


def shifted(value, axis, by):
    peers = lax.axis_size(axis)
    pairs = [(i, i + by) for i in range(peers) if 0 <= i + by < peers]
    return lax.ppermute(value, axis, pairs)


def block_increment(features, step_sizes, input_map, log_rates):
    cumulative = jnp.cumsum(log_rates, axis=1)
    to_end = jnp.exp(cumulative[:, -1:] - cumulative) * step_sizes
    weighted = (input_map[None, :, :] * to_end[:, :, None]).astype(jnp.bfloat16)
    increment = jnp.einsum("hsn,shp->hnp", weighted, features, preferred_element_type=jnp.float32)
    return (cumulative, increment)


def block_update(skip_gain, carry_state, inputs):
    features, step_sizes, input_map, output_map, log_rates = inputs
    cumulative, increment = block_increment(features, step_sizes, input_map, log_rates)
    length = log_rates.shape[1]
    row_index = lax.broadcasted_iota(jnp.int32, (length, length), 0)
    col_index = lax.broadcasted_iota(jnp.int32, (length, length), 1)
    causal = (row_index >= col_index)[None]
    log_gap = jnp.where(causal, cumulative[:, :, None] - cumulative[:, None, :], 0.0)
    decay_matrix = jnp.where(causal, jnp.exp(log_gap), 0.0)
    affinity = jnp.dot(
        output_map.astype(jnp.bfloat16),
        input_map.astype(jnp.bfloat16).T,
        preferred_element_type=jnp.float32,
    )
    weights = (affinity[None] * decay_matrix * step_sizes[:, None, :]).astype(jnp.bfloat16)
    inside = jnp.einsum("hts,shp->thp", weights, features, preferred_element_type=jnp.float32)
    entry_map = (output_map[None, :, :] * jnp.exp(cumulative)[:, :, None]).astype(jnp.bfloat16)
    carried = jnp.einsum(
        "htn,hnp->thp",
        entry_map,
        carry_state.astype(jnp.bfloat16),
        preferred_element_type=jnp.float32,
    )
    output = inside + carried + skip_gain[None, :, None] * features.astype(jnp.float32)
    following = jnp.exp(cumulative[:, -1])[:, None, None] * carry_state + increment
    return (following, output)


def split_blocks(features, step_sizes, input_map, output_map, log_rates):
    heads_here = step_sizes.shape[0]
    seq_rows = features.shape[0]
    blocks = seq_rows // BLOCK
    head_dim = features.shape[1] // heads_here
    feats_b = features.reshape(blocks, BLOCK, heads_here, head_dim)
    steps_b = step_sizes.reshape(heads_here, blocks, BLOCK).transpose(1, 0, 2)
    input_b = input_map.reshape(blocks, BLOCK, input_map.shape[1])
    output_b = output_map.reshape(blocks, BLOCK, output_map.shape[1])
    rates_b = log_rates.reshape(heads_here, blocks, BLOCK).transpose(1, 0, 2)
    return (feats_b, steps_b, input_b, output_b, rates_b)


def sequence_ssd(features, step_sizes, input_map, output_map, log_rates, skip_gain, entering):
    feats_b, steps_b, input_b, output_b, rates_b = split_blocks(
        features, step_sizes, input_map, output_map, log_rates
    )
    update = jax.checkpoint(partial(block_update, skip_gain))
    leaving, outputs = lax.scan(update, entering, (feats_b, steps_b, input_b, output_b, rates_b))
    return (outputs.reshape(features.shape[0], features.shape[1]), leaving)


def block_totals(feats_b, steps_b, input_b, rates_b, initial):

    def advance(carry_state, inputs):
        features, step_sizes, input_map, log_rates = inputs
        cumulative, increment = block_increment(features, step_sizes, input_map, log_rates)
        decay_last = jnp.exp(cumulative[:, -1])
        return (decay_last[:, None, None] * carry_state + increment, decay_last)

    final_state, decay_factors = lax.scan(advance, initial, (feats_b, steps_b, input_b, rates_b))
    return (final_state, jnp.prod(decay_factors, axis=0))


def entry_gradient(output_b, rates_b, grad_b, initial):
    cumulative = jnp.cumsum(rates_b, axis=2)
    entry_map = (output_b[:, None, :, :] * jnp.exp(cumulative)[:, :, :, None]).astype(jnp.bfloat16)
    pieces = jnp.einsum(
        "bhtn,bthp->bhnp", entry_map, grad_b, preferred_element_type=jnp.float32
    ).astype(jnp.bfloat16)
    pieces = lax.optimization_barrier(pieces).astype(jnp.float32)
    decay_factors = jnp.exp(cumulative[:, :, -1])

    def backward_step(accumulated, item):
        piece, decay_last = item
        return (piece + decay_last[:, None, None] * accumulated, decay_last)

    result, unused = lax.scan(backward_step, initial, (pieces, decay_factors), reverse=True)
    return result


def local(conv_input, conv_weight, conv_bias, step_size, log_decay, skip_gain, grad_output):
    taps_count = conv_weight.shape[0]
    tok_rows = conv_input.shape[0]
    earlier = shifted(conv_input[tok_rows - (taps_count - 1) :], ("ctx", "head"), 1)
    padded = jnp.concatenate([earlier, conv_input], axis=0).astype(jnp.float32)
    preact = conv_bias[None, :] + conv_weight[0][None, :] * padded[0:tok_rows]
    for offset in range(1, taps_count):
        preact = preact + conv_weight[offset][None, :] * padded[offset : offset + tok_rows]
    activated, silu_back = jax.vjp(jax.nn.silu, preact)
    activated = activated.astype(jnp.bfloat16)
    inner_width = activated.shape[1] - 2 * STATE
    head_feats = lax.all_to_all(
        activated[:, :inner_width], "head", split_axis=1, concat_axis=0, tiled=True
    )
    shared_maps = lax.all_gather(activated[:, inner_width:], "head", axis=0, tiled=True)
    input_map = shared_maps[:, :STATE].astype(jnp.float32)
    output_map = shared_maps[:, STATE:].astype(jnp.float32)
    heads_here = step_size.shape[0]
    head_dim = head_feats.shape[1] // heads_here
    feats_b, steps_b, input_b, output_b, rates_b = split_blocks(
        head_feats, step_size, input_map, output_map, log_decay
    )
    grad_b = grad_output.reshape(feats_b.shape)
    empty = jnp.zeros((heads_here, STATE, head_dim), jnp.float32)
    states_local, decay_total = block_totals(feats_b, steps_b, input_b, rates_b, empty)
    grad_local = entry_gradient(output_b, rates_b, grad_b, empty)

    def relay(rounds_done, state_pair):
        forward_state, backward_state = state_pair
        forward_state = shifted(decay_total[:, None, None] * forward_state + states_local, "ctx", 1)
        backward_state = shifted(
            decay_total[:, None, None] * backward_state + grad_local, "ctx", -1
        )
        return (forward_state, backward_state)

    entering, returning = lax.fori_loop(0, lax.axis_size("ctx") - 1, relay, (empty, empty))

    def local_part(features, steps_in, in_values, out_values, rates_in):
        return sequence_ssd(
            features, steps_in, in_values, out_values, rates_in, skip_gain, entering
        )

    (output_full, leaving), pullback = jax.vjp(
        local_part, head_feats, step_size, input_map, output_map, log_decay
    )
    grad_feats, grad_steps, grad_inmap, grad_outmap, grad_rates = pullback(
        (grad_output.astype(jnp.float32), returning)
    )
    map_grads = lax.psum_scatter(
        jnp.concatenate([grad_inmap, grad_outmap], axis=1), "head", scatter_dimension=0, tiled=True
    )
    back_feats = lax.all_to_all(grad_feats, "head", split_axis=0, concat_axis=1, tiled=True)
    grad_act = jnp.concatenate([back_feats, map_grads.astype(jnp.bfloat16)], axis=1).astype(
        jnp.float32
    )
    grad_pre = silu_back(grad_act)[0]
    following = shifted(grad_pre[: taps_count - 1], ("ctx", "head"), -1)
    extended = jnp.concatenate([grad_pre, following], axis=0)
    total = conv_weight[taps_count - 1][None, :] * extended[0:tok_rows]
    for offset in range(taps_count - 2, -1, -1):
        begin = taps_count - 1 - offset
        total = total + conv_weight[offset][None, :] * extended[begin : begin + tok_rows]
    return (output_full.astype(jnp.bfloat16), total.astype(jnp.bfloat16), grad_steps, grad_rates)


def solution(mesh):
    return jax.shard_map(
        local,
        mesh=mesh,
        in_specs=(
            P(("ctx", "head"), None),
            P(),
            P(),
            P("head", "ctx"),
            P("head", "ctx"),
            P("head"),
            P("ctx", "head"),
        ),
        out_specs=(P("ctx", "head"), P(("ctx", "head"), None), P("head", "ctx"), P("head", "ctx")),
        check_vma=False,
    )
```

profile of v0, /device:TPU:25, one launch (start us, length us, event | category | flops | bytes accessed | tf_op | source)
XLA Modules:
  0.0 897.2 jit_solution(15552508409402708683)
XLA Ops:
  8.7 3.7 collective-permute-start.2
  24.5 4.1 reshape.570
  28.6 6.8 reshape.571
  37.0 5.5 multiply_convert_fusion.44
  42.9 6.6 all_gather.3
  51.6 5.0 all-to-all-start
  58.1 6.0 fusion.136
  66.2 13.8 %while.86 = (s32[]{:T(128)}, f32[32,128,64]{2,1,0:T(8,128)}, f32[3,32,128,64]{2,3,1,0:T(8,128)}, f32[3,32]{1,0:T(4,128)S(1)}, s32[]{:T(128)}, /*index=5*/s32[]{:T(128)}, s32[]{:T(128)}) while((s32[]{:T(128)}, f32[32,128,64]{2,1,0:T(8,128)}, f32[3,32,128,64]{2,3,1,0:T(8,128)}, f32[3,32]{1,0:T(4,128)S(1)}, s32[]{:T(128)}, ...), condition=%wide.region_8.9_spmd.clone, body=%wide.region_7.8_spmd.clone.sunk | while | flops 786436 | bytes 7340523 | solution.py:101
  71.7 3.2 bitcast_add_fusion.3
  76.8 3.2 bitcast_add_fusion.3
  83.1 9.5 %all-to-all-done = bf16[192,4,2048]{2,0,1:T(8,128)(2,1)} async-done(((bf16[192,4,2048]{2,0,1:T(8,128)(2,1)}), bf16[192,4,2048]{2,0,1:T(8,128)(2,1)}, u32[]{:S(2)}, u32[]{:S(2)}) %all-to-all-start) | async-done | bytes 3145760 | tf_op jit(solution)/shard_map/all_to_all | solution.py:116
  92.7 10.1 %reshape.588 = bf16[3,256,32,64]{3,2,1,0:T(8,128)(2,1)} reshape(bf16[4,192,2048]{2,1,0:T(8,128)(2,1)} %bitcast.22) | data formatting | bytes 6291456 | tf_op jit(solution)/shard_map/reshape | solution.py:59
  102.7 6.9 copy.234
  109.7 18.4 %while.85 = (s32[]{:T(128)}, f32[32,128,64]{1,2,0:T(8,128)}, f32[3,32]{1,0:T(4,128)S(1)}, f32[3,32,256]{2,1,0:T(8,128)}, f32[3,256,128]{2,1,0:T(8,128)}, /*index...) while((s32[]{:T(128)}, f32[32,128,64]{1,2,0:T(8,128)}, ...), condition=%wide.region_3.4_spmd.clone, body=%wide.region_0.3_spmd.clone.sunk | while | flops 138174560 | bytes 4001547 | solution.py:84
  118.1 3.5 fusion.245
  124.5 3.5 fusion.245
  130.0 373.4 %while.82 = (s32[]{:T(128)}, f32[32,128,64]{1,2,0:T(8,128)S(1)}, f32[32,128,64]{1,2,0:T(8,128)S(1)}, f32[32]{0:T(128)S(1)}, f32[32,128,64]{1,2,0:T(8,128)}, /*index=5*/f32[32,128,64]{1,2,0:T(8,128)}, s32[]{:T(128)}) while((s32[]{:T(128)}, f32[32,128,64]{1,2,0:T(8,128)S(1)}, f32[32,128,64]{1,2,0:T(8,128)S(1)}, f32[32]{0:T(128)S(1)}, ...), condition=%wide.region_10.11_spmd, body=%wide.region_9.10_spmd.sunk | while | flops 1048578 | bytes 14680349 | solution.py:140
  135.0 4.0 collective-permute-start.1
  139.0 20.6 %collective-permute-done = f32[32,128,64]{1,2,0:T(8,128)S(1)} collective-permute-done((f32[32,128,64]{1,2,0:T(8,128)}, f32[32,128,64]{1,2,0:T(8,128)S(1)}, u32[]{:S(2)}, u32[]{:S(2)}) %collective-permute-start) | collective-permute-done | bytes 1048608 | tf_op jit(solution)/shard_map/while/body/eval_jaxpr/ppermute | solution.py:15
  159.6 23.7 %collective-permute-done.1 = f32[32,128,64]{1,2,0:T(8,128)S(1)} collective-permute-done((f32[32,128,64]{1,2,0:T(8,128)S(1)}, f32[32,128,64]{1,2,0:T(8,128)S(1)}, u32[]{:S(2)}, u32[]{:S(2)}) %collective-permute-start.1) | collective-permute-done | bytes 1048608 | tf_op jit(solution)/shard_map/while/body/eval_jaxpr/ppermute | solution.py:15
  188.0 4.3 collective-permute-start.1
  192.3 21.1 %collective-permute-done = f32[32,128,64]{1,2,0:T(8,128)S(1)} collective-permute-done((f32[32,128,64]{1,2,0:T(8,128)}, f32[32,128,64]{1,2,0:T(8,128)S(1)}, u32[]{:S(2)}, u32[]{:S(2)}) %collective-permute-start) | collective-permute-done | bytes 1048608 | tf_op jit(solution)/shard_map/while/body/eval_jaxpr/ppermute | solution.py:15
  213.4 23.3 %collective-permute-done.1 = f32[32,128,64]{1,2,0:T(8,128)S(1)} collective-permute-done((f32[32,128,64]{1,2,0:T(8,128)S(1)}, f32[32,128,64]{1,2,0:T(8,128)S(1)}, u32[]{:S(2)}, u32[]{:S(2)}) %collective-permute-start.1) | collective-permute-done | bytes 1048608 | tf_op jit(solution)/shard_map/while/body/eval_jaxpr/ppermute | solution.py:15
  241.4 4.3 collective-permute-start.1
  245.6 21.1 %collective-permute-done = f32[32,128,64]{1,2,0:T(8,128)S(1)} collective-permute-done((f32[32,128,64]{1,2,0:T(8,128)}, f32[32,128,64]{1,2,0:T(8,128)S(1)}, u32[]{:S(2)}, u32[]{:S(2)}) %collective-permute-start) | collective-permute-done | bytes 1048608 | tf_op jit(solution)/shard_map/while/body/eval_jaxpr/ppermute | solution.py:15
  266.7 23.3 %collective-permute-done.1 = f32[32,128,64]{1,2,0:T(8,128)S(1)} collective-permute-done((f32[32,128,64]{1,2,0:T(8,128)S(1)}, f32[32,128,64]{1,2,0:T(8,128)S(1)}, u32[]{:S(2)}, u32[]{:S(2)}) %collective-permute-start.1) | collective-permute-done | bytes 1048608 | tf_op jit(solution)/shard_map/while/body/eval_jaxpr/ppermute | solution.py:15
  294.7 4.3 collective-permute-start.1
  299.0 21.1 %collective-permute-done = f32[32,128,64]{1,2,0:T(8,128)S(1)} collective-permute-done((f32[32,128,64]{1,2,0:T(8,128)}, f32[32,128,64]{1,2,0:T(8,128)S(1)}, u32[]{:S(2)}, u32[]{:S(2)}) %collective-permute-start) | collective-permute-done | bytes 1048608 | tf_op jit(solution)/shard_map/while/body/eval_jaxpr/ppermute | solution.py:15
  320.1 23.3 %collective-permute-done.1 = f32[32,128,64]{1,2,0:T(8,128)S(1)} collective-permute-done((f32[32,128,64]{1,2,0:T(8,128)S(1)}, f32[32,128,64]{1,2,0:T(8,128)S(1)}, u32[]{:S(2)}, u32[]{:S(2)}) %collective-permute-start.1) | collective-permute-done | bytes 1048608 | tf_op jit(solution)/shard_map/while/body/eval_jaxpr/ppermute | solution.py:15
  348.0 4.3 collective-permute-start.1
  352.3 21.1 %collective-permute-done = f32[32,128,64]{1,2,0:T(8,128)S(1)} collective-permute-done((f32[32,128,64]{1,2,0:T(8,128)}, f32[32,128,64]{1,2,0:T(8,128)S(1)}, u32[]{:S(2)}, u32[]{:S(2)}) %collective-permute-start) | collective-permute-done | bytes 1048608 | tf_op jit(solution)/shard_map/while/body/eval_jaxpr/ppermute | solution.py:15
  373.4 23.3 %collective-permute-done.1 = f32[32,128,64]{1,2,0:T(8,128)S(1)} collective-permute-done((f32[32,128,64]{1,2,0:T(8,128)S(1)}, f32[32,128,64]{1,2,0:T(8,128)S(1)}, u32[]{:S(2)}, u32[]{:S(2)}) %collective-permute-start.1) | collective-permute-done | bytes 1048608 | tf_op jit(solution)/shard_map/while/body/eval_jaxpr/ppermute | solution.py:15
  401.4 4.3 collective-permute-start.1
  405.6 21.1 %collective-permute-done = f32[32,128,64]{1,2,0:T(8,128)S(1)} collective-permute-done((f32[32,128,64]{1,2,0:T(8,128)}, f32[32,128,64]{1,2,0:T(8,128)S(1)}, u32[]{:S(2)}, u32[]{:S(2)}) %collective-permute-start) | collective-permute-done | bytes 1048608 | tf_op jit(solution)/shard_map/while/body/eval_jaxpr/ppermute | solution.py:15
  426.7 23.3 %collective-permute-done.1 = f32[32,128,64]{1,2,0:T(8,128)S(1)} collective-permute-done((f32[32,128,64]{1,2,0:T(8,128)S(1)}, f32[32,128,64]{1,2,0:T(8,128)S(1)}, u32[]{:S(2)}, u32[]{:S(2)}) %collective-permute-start.1) | collective-permute-done | bytes 1048608 | tf_op jit(solution)/shard_map/while/body/eval_jaxpr/ppermute | solution.py:15
  454.7 4.3 collective-permute-start.1
  459.0 21.1 %collective-permute-done = f32[32,128,64]{1,2,0:T(8,128)S(1)} collective-permute-done((f32[32,128,64]{1,2,0:T(8,128)}, f32[32,128,64]{1,2,0:T(8,128)S(1)}, u32[]{:S(2)}, u32[]{:S(2)}) %collective-permute-start) | collective-permute-done | bytes 1048608 | tf_op jit(solution)/shard_map/while/body/eval_jaxpr/ppermute | solution.py:15
  480.1 23.3 %collective-permute-done.1 = f32[32,128,64]{1,2,0:T(8,128)S(1)} collective-permute-done((f32[32,128,64]{1,2,0:T(8,128)S(1)}, f32[32,128,64]{1,2,0:T(8,128)S(1)}, u32[]{:S(2)}, u32[]{:S(2)}) %collective-permute-start.1) | collective-permute-done | bytes 1048608 | tf_op jit(solution)/shard_map/while/body/eval_jaxpr/ppermute | solution.py:15
  503.3 44.6 %while.84 = (s32[]{:T(128)}, f32[32,128,64]{1,2,0:T(8,128)S(1)}, bf16[3,256,32,64]{1,3,2,0:T(8,128)(2,1)}, f32[3,32,128,64]{2,3,1,0:T(8,128)}, f32[3,32,256]{2,1...) while((s32[]{:T(128)}, f32[32,128,64]{1,2,0:T(8,128)S(1)}, ...), condition=%wide.region_14.15_spmd.clone.clone, body=%wide.region_11.14_spmd.clone.clone.sunk | while | flops 574382208 | bytes 54597228 | solution.py:72
  506.5 4.0 fusion.243
  521.4 4.0 fusion.243
  536.3 4.0 fusion.243
  552.9 229.2 %while.83 = (s32[]{:T(128)}, f32[32,128,64]{1,2,0:T(8,128)S(1)}, bf16[3,256,32,64]{1,3,2,0:T(8,128)(2,1)}, f32[3,32,256]{2,1,0:T(8,128)}, f32[3,256,128]{2,1,0:T...) while((s32[]{:T(128)}, f32[32,128,64]{1,2,0:T(8,128)S(1)}, ...), condition=%wide.region_30.31_spmd, body=%wide.region_15.30_spmd.sunk | while | flops 1193058432 | bytes 43096368 | solution.py:72
  553.1 5.6 constant_dynamic-slice_fusion.17
  589.3 8.6 fusion.231
  610.7 3.8 reduce-window.96
  622.7 4.3 fusion.229
  629.4 5.6 constant_dynamic-slice_fusion.17
  665.6 8.6 fusion.231
  687.1 3.8 reduce-window.96
  699.0 4.3 fusion.229
  705.8 5.6 constant_dynamic-slice_fusion.17
  742.0 8.6 fusion.231
  763.4 3.8 reduce-window.96
  775.4 4.3 fusion.229
  782.1 10.5 %copy.263 = bf16[3,256,32,64]{3,2,1,0:T(8,128)(2,1)} copy(bf16[3,256,32,64]{1,3,2,0:T(8,128)(2,1)} %get-tuple-element.606) | data formatting | bytes 6291456 | tf_op jit(solution)/shard_map/all_to_all | solution.py:156
  792.6 9.7 %reshape.587 = bf16[4,192,2048]{2,1,0:T(8,128)(2,1)} reshape(bf16[3,256,32,64]{3,2,1,0:T(8,128)(2,1)} %copy.263) | data formatting | bytes 6291456 | tf_op jit(solution)/shard_map/all_to_all | solution.py:156
  802.3 4.3 all-to-all-start.1
  808.6 29.7 %reduce-scatter.2.cloned.1.call-done = f32[192,256]{1,0:T(8,128)} async-done(((f32[768,256]{1,0:T(8,128)}), f32[192,256]{1,0:T(8,128)}) %reduce-scatter.2.cloned.1.call-update) | async-done | bytes 196624 | tf_op jit(solution)/shard_map/reduce_scatter | solution.py:153
  839.2 7.6 all-to-all-done.1
  847.3 4.5 fusion.125
  858.6 9.5 %copy.262 = bf16[3,256,32,64]{3,2,1,0:T(8,128)(2,1)} copy(bf16[3,256,32,64]{1,3,2,0:T(8,128)(2,1)S(1)} %copy-done.12) | data formatting | bytes 6291456
  868.1 9.8 %reshape.586 = bf16[768,2048]{1,0:T(8,128)(2,1)} reshape(bf16[3,256,32,64]{3,2,1,0:T(8,128)(2,1)} %copy.262) | data formatting | bytes 6291456
  877.9 12.0 %fusion.121 = bf16[192,8448]{1,0:T(8,128)(2,1)} fusion(f32[192,8448]{1,0:T(8,128)} %copy-done.3, f32[3,8448]{1,0:T(4,128)S(1)} %collective-permute-done.3, f32[8448]{0:T(1024)S(1)} %copy-done.22, f32[8448]{0:T(1024)S(1)} %copy-done.24, f32[8448]{0:T(1024)S(1)} %copy-done.20, f32[8448]{0:T(1024)S(1)} %copy-done.18), kind=kLoop, calls=%fused_computation.183 | loop fusion | flops 17842176 | bytes 9968640 | tf_op jit(solution)/shard_map/convert_element_type | solution.py:167
  (409 shorter events, 286.8 us)
Async XLA Ops:
  8.7 26.7 %collective-permute-start.2 = (bf16[3,8448]{1,0:T(4,128)(2,1)}, bf16[3,8448]{1,0:T(4,128)(2,1)}, u32[]{:S(2)}, u32[]{:S(2)}) collective-permute-start(bf16[3,8448]{1,0:T(4,128)(2,1)} %slice.138), channel_id=1, source_target_pairs={{0,1},{1,2},{2,3},{3,4},{4,5},{5,6},{6,7},{7,8},{8,9},{9,10},{10,1... | collective-permute-start | bytes 152072 | tf_op jit(solution)/shard_map/ppermute | solution.py:15
  17.3 19.7 %copy-start.17 = (f32[8448]{0:T(1024)}, f32[8448]{0:T(1024)S(1)}, u32[]{:S(2)}) copy-start(f32[8448]{0:T(1024)S(1)} %get-tuple-element.982) | copy-start | bytes 101380
  17.3 19.7 %copy-start.19 = (f32[8448]{0:T(1024)}, f32[8448]{0:T(1024)S(1)}, u32[]{:S(2)}) copy-start(f32[8448]{0:T(1024)S(1)} %get-tuple-element.983) | copy-start | bytes 101380
  17.3 19.7 %copy-start.21 = (f32[8448]{0:T(1024)}, f32[8448]{0:T(1024)S(1)}, u32[]{:S(2)}) copy-start(f32[8448]{0:T(1024)S(1)} %get-tuple-element.984) | copy-start | bytes 101380
  17.3 19.7 %copy-start.23 = (f32[8448]{0:T(1024)}, f32[8448]{0:T(1024)S(1)}, u32[]{:S(2)}) copy-start(f32[8448]{0:T(1024)S(1)} %get-tuple-element.985) | copy-start | bytes 101380
  28.6 6.8 copy-start.7
  35.4 1.6 copy-start.26
  51.6 41.1 %all-to-all-start = ((bf16[192,4,2048]{2,0,1:T(8,128)(2,1)}), bf16[192,4,2048]{2,0,1:T(8,128)(2,1)}, u32[]{:S(2)}, u32[]{:S(2)}) async-start(bf16[192,4,2048]{2,0,1:T(8,128)(2,1)} %bitcast.218), calls=%async_computation | async-start | bytes 6291456 | tf_op jit(solution)/shard_map/all_to_all | solution.py:116
  128.0 1.7 copy-start
  129.9 373.4 %copy-start.25 = (pred[256,256]{1,0:T(8,128)(4,1)S(1)}, pred[256,256]{1,0:T(8,128)(4,1)}, u32[]{:S(2)}) copy-start(pred[256,256]{1,0:T(8,128)(4,1)} %iota_compare_fusion.1) | copy-start | bytes 196612
  132.8 26.8 %collective-permute-start = (f32[32,128,64]{1,2,0:T(8,128)}, f32[32,128,64]{1,2,0:T(8,128)S(1)}, u32[]{:S(2)}, u32[]{:S(2)}) collective-permute-start(f32[32,128,64]{1,2,0:T(8,128)} %get-tuple-element.1349), channel_id=1, source_target_pairs={{0,4},{4,8},{8,12},{12,16},{16,20},{20,24},{24,28},{1,5},{5,9},{9,... | collective-permute-start | bytes 3145736 | tf_op jit(solution)/shard_map/while/body/eval_jaxpr/ppermute | solution.py:15
  135.0 48.4 %collective-permute-start.1 = (f32[32,128,64]{1,2,0:T(8,128)S(1)}, f32[32,128,64]{1,2,0:T(8,128)S(1)}, u32[]{:S(2)}, u32[]{:S(2)}) collective-permute-start(f32[32,128,64]{1,2,0:T(8,128)S(1)} %get-tuple-element.1350), channel_id=1, source_target_pairs={{4,0},{8,4},{12,8},{16,12},{20,16},{24,20},{28,24},{5,1},{9,5},{13... | collective-permute-start | bytes 3145736 | tf_op jit(solution)/shard_map/while/body/eval_jaxpr/ppermute | solution.py:15
  186.1 27.3 %collective-permute-start = (f32[32,128,64]{1,2,0:T(8,128)}, f32[32,128,64]{1,2,0:T(8,128)S(1)}, u32[]{:S(2)}, u32[]{:S(2)}) collective-permute-start(f32[32,128,64]{1,2,0:T(8,128)} %get-tuple-element.1349), channel_id=1, source_target_pairs={{0,4},{4,8},{8,12},{12,16},{16,20},{20,24},{24,28},{1,5},{5,9},{9,... | collective-permute-start | bytes 3145736 | tf_op jit(solution)/shard_map/while/body/eval_jaxpr/ppermute | solution.py:15
  188.0 48.6 %collective-permute-start.1 = (f32[32,128,64]{1,2,0:T(8,128)S(1)}, f32[32,128,64]{1,2,0:T(8,128)S(1)}, u32[]{:S(2)}, u32[]{:S(2)}) collective-permute-start(f32[32,128,64]{1,2,0:T(8,128)S(1)} %get-tuple-element.1350), channel_id=1, source_target_pairs={{4,0},{8,4},{12,8},{16,12},{20,16},{24,20},{28,24},{5,1},{9,5},{13... | collective-permute-start | bytes 3145736 | tf_op jit(solution)/shard_map/while/body/eval_jaxpr/ppermute | solution.py:15
  239.5 27.3 %collective-permute-start = (f32[32,128,64]{1,2,0:T(8,128)}, f32[32,128,64]{1,2,0:T(8,128)S(1)}, u32[]{:S(2)}, u32[]{:S(2)}) collective-permute-start(f32[32,128,64]{1,2,0:T(8,128)} %get-tuple-element.1349), channel_id=1, source_target_pairs={{0,4},{4,8},{8,12},{12,16},{16,20},{20,24},{24,28},{1,5},{5,9},{9,... | collective-permute-start | bytes 3145736 | tf_op jit(solution)/shard_map/while/body/eval_jaxpr/ppermute | solution.py:15
  241.4 48.6 %collective-permute-start.1 = (f32[32,128,64]{1,2,0:T(8,128)S(1)}, f32[32,128,64]{1,2,0:T(8,128)S(1)}, u32[]{:S(2)}, u32[]{:S(2)}) collective-permute-start(f32[32,128,64]{1,2,0:T(8,128)S(1)} %get-tuple-element.1350), channel_id=1, source_target_pairs={{4,0},{8,4},{12,8},{16,12},{20,16},{24,20},{28,24},{5,1},{9,5},{13... | collective-permute-start | bytes 3145736 | tf_op jit(solution)/shard_map/while/body/eval_jaxpr/ppermute | solution.py:15
  292.8 27.3 %collective-permute-start = (f32[32,128,64]{1,2,0:T(8,128)}, f32[32,128,64]{1,2,0:T(8,128)S(1)}, u32[]{:S(2)}, u32[]{:S(2)}) collective-permute-start(f32[32,128,64]{1,2,0:T(8,128)} %get-tuple-element.1349), channel_id=1, source_target_pairs={{0,4},{4,8},{8,12},{12,16},{16,20},{20,24},{24,28},{1,5},{5,9},{9,... | collective-permute-start | bytes 3145736 | tf_op jit(solution)/shard_map/while/body/eval_jaxpr/ppermute | solution.py:15
  294.7 48.6 %collective-permute-start.1 = (f32[32,128,64]{1,2,0:T(8,128)S(1)}, f32[32,128,64]{1,2,0:T(8,128)S(1)}, u32[]{:S(2)}, u32[]{:S(2)}) collective-permute-start(f32[32,128,64]{1,2,0:T(8,128)S(1)} %get-tuple-element.1350), channel_id=1, source_target_pairs={{4,0},{8,4},{12,8},{16,12},{20,16},{24,20},{28,24},{5,1},{9,5},{13... | collective-permute-start | bytes 3145736 | tf_op jit(solution)/shard_map/while/body/eval_jaxpr/ppermute | solution.py:15
  346.1 27.3 %collective-permute-start = (f32[32,128,64]{1,2,0:T(8,128)}, f32[32,128,64]{1,2,0:T(8,128)S(1)}, u32[]{:S(2)}, u32[]{:S(2)}) collective-permute-start(f32[32,128,64]{1,2,0:T(8,128)} %get-tuple-element.1349), channel_id=1, source_target_pairs={{0,4},{4,8},{8,12},{12,16},{16,20},{20,24},{24,28},{1,5},{5,9},{9,... | collective-permute-start | bytes 3145736 | tf_op jit(solution)/shard_map/while/body/eval_jaxpr/ppermute | solution.py:15
  348.0 48.6 %collective-permute-start.1 = (f32[32,128,64]{1,2,0:T(8,128)S(1)}, f32[32,128,64]{1,2,0:T(8,128)S(1)}, u32[]{:S(2)}, u32[]{:S(2)}) collective-permute-start(f32[32,128,64]{1,2,0:T(8,128)S(1)} %get-tuple-element.1350), channel_id=1, source_target_pairs={{4,0},{8,4},{12,8},{16,12},{20,16},{24,20},{28,24},{5,1},{9,5},{13... | collective-permute-start | bytes 3145736 | tf_op jit(solution)/shard_map/while/body/eval_jaxpr/ppermute | solution.py:15
  399.5 27.3 %collective-permute-start = (f32[32,128,64]{1,2,0:T(8,128)}, f32[32,128,64]{1,2,0:T(8,128)S(1)}, u32[]{:S(2)}, u32[]{:S(2)}) collective-permute-start(f32[32,128,64]{1,2,0:T(8,128)} %get-tuple-element.1349), channel_id=1, source_target_pairs={{0,4},{4,8},{8,12},{12,16},{16,20},{20,24},{24,28},{1,5},{5,9},{9,... | collective-permute-start | bytes 3145736 | tf_op jit(solution)/shard_map/while/body/eval_jaxpr/ppermute | solution.py:15
  401.4 48.6 %collective-permute-start.1 = (f32[32,128,64]{1,2,0:T(8,128)S(1)}, f32[32,128,64]{1,2,0:T(8,128)S(1)}, u32[]{:S(2)}, u32[]{:S(2)}) collective-permute-start(f32[32,128,64]{1,2,0:T(8,128)S(1)} %get-tuple-element.1350), channel_id=1, source_target_pairs={{4,0},{8,4},{12,8},{16,12},{20,16},{24,20},{28,24},{5,1},{9,5},{13... | collective-permute-start | bytes 3145736 | tf_op jit(solution)/shard_map/while/body/eval_jaxpr/ppermute | solution.py:15
  452.8 27.3 %collective-permute-start = (f32[32,128,64]{1,2,0:T(8,128)}, f32[32,128,64]{1,2,0:T(8,128)S(1)}, u32[]{:S(2)}, u32[]{:S(2)}) collective-permute-start(f32[32,128,64]{1,2,0:T(8,128)} %get-tuple-element.1349), channel_id=1, source_target_pairs={{0,4},{4,8},{8,12},{12,16},{16,20},{20,24},{24,28},{1,5},{5,9},{9,... | collective-permute-start | bytes 3145736 | tf_op jit(solution)/shard_map/while/body/eval_jaxpr/ppermute | solution.py:15
  454.7 48.6 %collective-permute-start.1 = (f32[32,128,64]{1,2,0:T(8,128)S(1)}, f32[32,128,64]{1,2,0:T(8,128)S(1)}, u32[]{:S(2)}, u32[]{:S(2)}) collective-permute-start(f32[32,128,64]{1,2,0:T(8,128)S(1)} %get-tuple-element.1350), channel_id=1, source_target_pairs={{4,0},{8,4},{12,8},{16,12},{20,16},{24,20},{28,24},{5,1},{9,5},{13... | collective-permute-start | bytes 3145736 | tf_op jit(solution)/shard_map/while/body/eval_jaxpr/ppermute | solution.py:15
  506.5 5.0 copy-start.1
  506.5 5.0 copy-start.10
  513.9 1.7 copy-start.11
  521.4 5.0 copy-start.1
  521.4 5.0 copy-start.10
  528.8 1.7 copy-start.11
  536.3 5.0 copy-start.1
  536.3 5.0 copy-start.10
  543.8 1.7 copy-start.11
  589.2 8.6 copy-start.13
  589.2 9.3 %copy-start.2 = (f32[1,256,128]{1,2,0:T(8,128)S(1)}, f32[1,256,128]{1,2,0:T(8,128)}, u32[]{:S(2)}) copy-start(f32[1,256,128]{1,2,0:T(8,128)} %copy.332) | copy-start | bytes 393220 | tf_op jit(solution)/shard_map/transpose(jvp())/while
  589.3 9.3 %copy-start.5 = (f32[256,128]{1,0:T(8,128)S(1)}, f32[256,128]{1,0:T(8,128)}, u32[]{:S(2)}) copy-start(f32[256,128]{1,0:T(8,128)} %copy.347) | copy-start | bytes 393220 | tf_op jit(solution)/shard_map/transpose(jvp())/while
  597.9 0.7 copy-start.4
  622.7 4.4 copy-start.8
  622.7 5.9 copy-start.9
  665.6 8.6 copy-start.13
  665.6 9.3 %copy-start.2 = (f32[1,256,128]{1,2,0:T(8,128)S(1)}, f32[1,256,128]{1,2,0:T(8,128)}, u32[]{:S(2)}) copy-start(f32[1,256,128]{1,2,0:T(8,128)} %copy.332) | copy-start | bytes 393220 | tf_op jit(solution)/shard_map/transpose(jvp())/while
  665.6 9.3 %copy-start.5 = (f32[256,128]{1,0:T(8,128)S(1)}, f32[256,128]{1,0:T(8,128)}, u32[]{:S(2)}) copy-start(f32[256,128]{1,0:T(8,128)} %copy.347) | copy-start | bytes 393220 | tf_op jit(solution)/shard_map/transpose(jvp())/while
  674.2 0.7 copy-start.4
  699.0 4.4 copy-start.8
  699.0 5.9 copy-start.9
  722.9 0.6 copy-start.6
  741.9 8.6 copy-start.13
  742.0 9.3 %copy-start.2 = (f32[1,256,128]{1,2,0:T(8,128)S(1)}, f32[1,256,128]{1,2,0:T(8,128)}, u32[]{:S(2)}) copy-start(f32[1,256,128]{1,2,0:T(8,128)} %copy.332) | copy-start | bytes 393220 | tf_op jit(solution)/shard_map/transpose(jvp())/while
  742.0 9.3 %copy-start.5 = (f32[256,128]{1,0:T(8,128)S(1)}, f32[256,128]{1,0:T(8,128)}, u32[]{:S(2)}) copy-start(f32[256,128]{1,0:T(8,128)} %copy.347) | copy-start | bytes 393220 | tf_op jit(solution)/shard_map/transpose(jvp())/while
  750.6 0.7 copy-start.4
  775.4 4.4 copy-start.8
  775.4 5.9 copy-start.9
  802.3 4.3 copy-start.14
  802.3 44.6 %all-to-all-start.1 = ((bf16[4,192,2048]{2,1,0:T(8,128)(2,1)}), bf16[4,192,2048]{2,1,0:T(8,128)(2,1)S(1)}, u32[]{:S(2)}, u32[]{:S(2)}) async-start(bf16[4,192,2048]{2,1,0:T(8,128)(2,1)} %reshape.587), calls=%async_computation.1 | async-start | bytes 6291456 | tf_op jit(solution)/shard_map/all_to_all | solution.py:156
  806.6 31.7 %reduce-scatter.2.cloned.1.call-start = ((), (), s32[]{:S(2)}) async-start(), calls=%async_computation.3 | async-start | bytes 983040 | tf_op jit(solution)/shard_map/reduce_scatter | solution.py:153
  847.3 10.1 %copy-start.15 = (f32[3,32,256]{2,1,0:T(8,128)S(1)}, f32[3,32,256]{2,1,0:T(8,128)}, u32[]{:S(2)}) copy-start(f32[3,32,256]{2,1,0:T(8,128)} %get-tuple-element.609) | copy-start | bytes 294916
  847.3 10.7 %copy-start.16 = (f32[3,32,256]{2,1,0:T(8,128)S(1)}, f32[3,32,256]{2,1,0:T(8,128)}, u32[]{:S(2)}) copy-start(f32[3,32,256]{2,1,0:T(8,128)} %get-tuple-element.610) | copy-start | bytes 294916
  847.3 11.3 %copy-start.12 = (bf16[3,256,32,64]{1,3,2,0:T(8,128)(2,1)S(1)}, bf16[3,256,32,64]{1,3,2,0:T(8,128)(2,1)}, u32[]{:S(2)}) copy-start(bf16[3,256,32,64]{1,3,2,0:T(8,128)(2,1)} %get-tuple-element.603) | copy-start | bytes 9437188
  851.8 2.7 copy-start.3
  854.5 23.3 %collective-permute-start.3 = (f32[3,8448]{1,0:T(4,128)S(1)}, f32[3,8448]{1,0:T(4,128)S(1)}, u32[]{:S(2)}, u32[]{:S(2)}) collective-permute-start(f32[3,8448]{1,0:T(4,128)S(1)} %slice.184), channel_id=1, source_target_pairs={{1,0},{2,1},{3,2},{4,3},{5,4},{6,5},{7,6},{8,7},{9,8},{10,9},{11,1... | collective-permute-start | bytes 304136 | tf_op jit(solution)/shard_map/ppermute | solution.py:15
  868.1 9.8 %copy-start.18 = (f32[8448]{0:T(1024)S(1)}, f32[8448]{0:T(1024)}, u32[]{:S(2)}) copy-start(f32[8448]{0:T(1024)} %copy-done.17) | copy-start | bytes 101380
  868.1 9.8 %copy-start.20 = (f32[8448]{0:T(1024)S(1)}, f32[8448]{0:T(1024)}, u32[]{:S(2)}) copy-start(f32[8448]{0:T(1024)} %copy-done.19) | copy-start | bytes 101380
  868.1 9.8 %copy-start.22 = (f32[8448]{0:T(1024)S(1)}, f32[8448]{0:T(1024)}, u32[]{:S(2)}) copy-start(f32[8448]{0:T(1024)} %copy-done.21) | copy-start | bytes 101380
  868.1 9.8 %copy-start.24 = (f32[8448]{0:T(1024)S(1)}, f32[8448]{0:T(1024)}, u32[]{:S(2)}) copy-start(f32[8448]{0:T(1024)} %copy-done.23) | copy-start | bytes 101380
  (2 other events, 1.2 us)
Sparse Core Ops, SparseCore 0:
  810.5 27.7 reduce-scatter.1
where the time goes:
time: 909 us; the launch traced here: 897 us
  waiting for transfers between devices  357 us (39%)
  local copies, waits for them, and re-layouts  225 us (25%)
  matrix products  119 us (13%)
  other arithmetic  114 us (13%)
  starting transfers between devices  58.9 us (6%)
  between operations  14.8 us (2%)
    ppermute x16, waiting for transfers between devices, shifted(): return lax.ppermute(value, axis, pairs)  311 us
    dot_general x9, matrix products, block_update(): jnp.einsum('hts,shp->thp', weights, features, preferred_element_type=jnp....  50.8 us
    ppermute x16, starting transfers between devices, shifted(): return lax.ppermute(value, axis, pairs)  49.6 us
    unnamed x40, local copies, waits for them, and re-layouts  35.3 us
    reduce_scatter x1, waiting for transfers between devices, local(): lax.psum_scatter(jnp.concatenate([grad_inmap, grad_outmap], axis=1), 'hea...  29.7 us
    dot_general x12, matrix products, block_increment(): jnp.einsum('hsn,shp->hnp', weighted, features, preferred_element_type=jnp...  27.1 us
    another operation x59, local copies, waits for them, and re-layouts  26.7 us
    another operation x42, other arithmetic  26.6 us
  transfers between devices with their start and end apart: 19, of which 17 were waited for; matrix products, arithmetic and copies ran while one was open for 8% of the time, Pallas kernels for 0%

commit v1 on v0

v1 whole, which is shorter than its diff:
```python
from functools import partial

import jax
import jax.numpy as jnp
from jax import lax
from jax.experimental import pallas as pl
from jax.experimental.pallas import tpu as pltpu
from jax.sharding import PartitionSpec as P

STATE = 128
BLOCK = 256
GROUP = 8
F32 = jnp.float32
BF16 = jnp.bfloat16
VMEM_LIMIT = 50 * 1024 * 1024


def dot(a, b, ca, cb, precision=None):
    return lax.dot_general(
        a, b, (((ca,), (cb,)), ((), ())), precision=precision, preferred_element_type=F32
    )


def halves(value):
    high = value.astype(BF16)
    return high, (value - high.astype(F32)).astype(BF16)


def head_of_lane(rows, width, head_dim):
    row = lax.broadcasted_iota(jnp.int32, (rows, width), 0)
    lane = lax.broadcasted_iota(jnp.int32, (rows, width), 1)
    return jnp.where(lax.rem(row, GROUP) == lane // head_dim, 1.0, 0.0).astype(BF16)


def expand(rows, width, head_dim):
    high = rows.astype(BF16).astype(F32)
    both = jnp.concatenate([high, rows - high], axis=0).astype(BF16)
    return dot(both, head_of_lane(2 * GROUP, width, head_dim), 0, 0)


def head_sums(value, head_dim):
    pick = head_of_lane(GROUP, value.shape[1], head_dim)
    high, low = halves(value)
    return dot(pick, high, 1, 1) + dot(pick, low, 1, 1)


def earlier_or_same(length):
    row = lax.broadcasted_iota(jnp.int32, (length, length), 0)
    col = lax.broadcasted_iota(jnp.int32, (length, length), 1)
    return jnp.where(row <= col, 1.0, 0.0)


def running_sum(rates):
    return dot(rates, earlier_or_same(rates.shape[1]), 1, 0, lax.Precision.HIGHEST)


def states_kernel(head_dim, x_ref, m_ref, dy_ref, rate_ref, step_ref, inc_ref, gp_ref, dec_ref, pack_ref, t_ref, r_ref, d_ref):
    b = pl.program_id(1)
    width = x_ref.shape[1]
    cum = running_sum(rate_ref[...])
    last = cum[:, BLOCK - 1 :]
    to_end = expand(jnp.exp(last - cum) * step_ref[...], width, head_dim)
    from_start = expand(jnp.exp(cum), width, head_dim)
    xw = (x_ref[...].astype(F32) * to_end).astype(BF16)
    dyw = (dy_ref[...].astype(F32) * from_start).astype(BF16)
    inc = dot(m_ref[:, :STATE], xw, 0, 0)
    gp = dot(m_ref[:, STATE:], dyw, 0, 0)
    dec = from_start[BLOCK - 1 :]
    inc_ref[0] = inc
    gp_ref[0] = gp
    dec_ref[0] = jnp.broadcast_to(dec, (GROUP, width))

    @pl.when(b == 0)
    def _():
        t_ref[...] = inc
        r_ref[...] = gp
        d_ref[...] = jnp.broadcast_to(dec, d_ref.shape)

    @pl.when(b > 0)
    def _():
        t_ref[...] = t_ref[...] * dec + inc
        r_ref[...] = r_ref[...] + d_ref[0:1] * gp
        d_ref[...] = d_ref[...] * dec

    @pl.when(b == pl.num_programs(1) - 1)
    def _():
        decay = d_ref[...]
        high = decay.astype(BF16).astype(F32)
        both = jnp.concatenate([high, decay - high], axis=0).astype(BF16)
        pieces, rows, part = pack_ref.shape
        for i in range(pieces):
            lanes = slice(i * part, (i + 1) * part)
            pack_ref[i, :STATE] = t_ref[:, lanes].astype(BF16)
            pack_ref[i, STATE : 2 * STATE] = r_ref[:, lanes].astype(BF16)
            pack_ref[i, 2 * STATE :] = both[:, lanes]


def chain_kernel(in_ref, out_ref):
    peers, rows, part = in_ref.shape

    def decay(c):
        return in_ref[c, 2 * STATE : 2 * STATE + 1].astype(F32) + in_ref[
            c, 2 * STATE + GROUP : 2 * STATE + GROUP + 1
        ].astype(F32)

    state = jnp.zeros((STATE, part), F32)
    for c in range(peers):
        out_ref[c, :STATE] = state.astype(BF16)
        state = decay(c) * state + in_ref[c, :STATE].astype(F32)
    grad = jnp.zeros((STATE, part), F32)
    for c in range(peers - 1, -1, -1):
        out_ref[c, STATE:] = grad.astype(BF16)
        grad = decay(c) * grad + in_ref[c, STATE : 2 * STATE].astype(F32)


def intra_kernel(head_dim, x_ref, m_ref, dy_ref, rate_ref, step_ref, skip_ref, y_ref, dx_ref, gs_ref, gc_ref, gm_ref, aff_ref, da_ref):
    g = pl.program_id(1)
    width = x_ref.shape[1]
    row = lax.broadcasted_iota(jnp.int32, (BLOCK, BLOCK), 0)
    col = lax.broadcasted_iota(jnp.int32, (BLOCK, BLOCK), 1)
    causal = row >= col

    @pl.when(g == 0)
    def _():
        aff_ref[...] = jnp.where(causal, dot(m_ref[:, STATE:], m_ref[:, :STATE], 1, 1), 0.0)
        da_ref[...] = jnp.zeros_like(da_ref)

    cum = running_sum(rate_ref[...])
    cum_col = cum.T
    x = x_ref[...].astype(F32)
    dy = dy_ref[...]
    steps = expand(step_ref[...], width, head_dim)
    xs = (x * steps).astype(BF16)
    pair = 2 * head_dim
    lane = lax.broadcasted_iota(jnp.int32, (BLOCK, pair), 1)
    ins_parts, back_parts = [], []
    for p in range(GROUP // 2):
        lanes = slice(p * pair, (p + 1) * pair)
        xs_p, dy_p = xs[:, lanes], dy[:, lanes]
        ins, back = 0.0, 0.0
        for k in range(2):
            h = 2 * p + k
            mine = (lane // head_dim) == k
            xs_h = jnp.where(mine, xs_p, jnp.zeros_like(xs_p))
            dy_h = jnp.where(mine, dy_p, jnp.zeros_like(dy_p))
            decay = jnp.exp(jnp.minimum(cum_col[:, h : h + 1] - cum[h : h + 1, :], 0.0))
            weights = (aff_ref[...] * decay).astype(BF16)
            ins = ins + dot(weights, xs_h, 1, 0)
            back = back + dot(weights, dy_h, 0, 0)
            da_ref[...] += dot(dy_h, xs_p, 1, 1) * decay
        ins_parts.append(ins)
        back_parts.append(back)
    ins = jnp.concatenate(ins_parts, axis=1)
    back = jnp.concatenate(back_parts, axis=1)
    skip = skip_ref[0:1]
    dyf = dy.astype(F32)
    y_ref[...] = (ins + skip * x).astype(BF16)
    dx_ref[...] = (steps * back + skip * dyf).astype(BF16)
    gs_ref[...] = head_sums(x * back, head_dim)
    gc_ref[...] = head_sums(dyf * ins, head_dim) - head_sums(xs.astype(F32) * back, head_dim)

    @pl.when(g == pl.num_programs(1) - 1)
    def _():
        da = jnp.where(causal, da_ref[...], 0.0).astype(BF16)
        gm_ref[:, :STATE] = dot(da, m_ref[:, STATE:], 0, 0)
        gm_ref[:, STATE:] = dot(da, m_ref[:, :STATE], 1, 0)


def carry_kernel(head_dim, x_ref, m_ref, dy_ref, rate_ref, step_ref, y1_ref, dx1_ref, gs1_ref, gc1_ref, gm1_ref,
                 inc_ref, gp_ref, dec_ref, enter_ref, y_ref, dx_ref, gs_ref, gd_ref, s_ref, g_ref, dot_ref, acc_ref):
    b, g = pl.program_id(0), pl.program_id(1)
    width = x_ref.shape[1]
    blocks = inc_ref.shape[0]

    @pl.when(b == 0)
    def _():
        pieces = enter_ref.shape[0]
        state = jnp.concatenate([enter_ref[i, :STATE] for i in range(pieces)], axis=1).astype(F32)
        grad = jnp.concatenate([enter_ref[i, STATE:] for i in range(pieces)], axis=1).astype(F32)
        grads = [None] * blocks
        for k in range(blocks - 1, -1, -1):
            grads[k] = grad
            g_ref[k, g] = grad.astype(BF16)
            if k > 0:
                grad = dec_ref[k, 0:1] * grad + gp_ref[k]
        for k in range(blocks):
            s_ref[k, g] = state.astype(BF16)
            state = dec_ref[k, 0:1] * state + inc_ref[k]
            total = jnp.sum(state * grads[k], axis=0, keepdims=True)
            total = jnp.broadcast_to(total, (128, width))
            dot_ref[k, g] = head_sums(total, head_dim)

    cum = running_sum(rate_ref[...])
    ending = jnp.exp(cum[:, BLOCK - 1 :] - cum)
    weight = ending * step_ref[...]
    from_start = expand(jnp.exp(cum), width, head_dim)
    to_end = expand(weight, width, head_dim)
    x = x_ref[...].astype(F32)
    dy = dy_ref[...].astype(F32)
    state, grad = s_ref[b, g], g_ref[b, g]
    in_map, out_map = m_ref[:, :STATE], m_ref[:, STATE:]
    carried = from_start * dot(out_map, state, 1, 0)
    pulled = dot(in_map, grad, 1, 0)
    y_ref[...] = (y1_ref[...].astype(F32) + carried).astype(BF16)
    dx = (dx1_ref[...].astype(F32) + to_end * pulled).astype(BF16)
    lanes = pl.ds(pl.multiple_of(g * width, width), width)
    dx_ref[:, lanes] = dx
    xq = head_sums(x * pulled, head_dim)
    gs_ref[...] = gs1_ref[...] + ending * xq
    gc = gc1_ref[...] + head_sums(dy * carried, head_dim) - weight * xq
    at = lax.broadcasted_iota(jnp.int32, gc.shape, 1)
    gc = gc + jnp.where(at == BLOCK - 1, dot_ref[b, g][:, 0:1], 0.0)
    gd_ref[...] = dot(gc, earlier_or_same(BLOCK), 1, 1, lax.Precision.HIGHEST)
    d_in = dot((x * to_end).astype(BF16), grad, 1, 1)
    d_out = dot((dy * from_start).astype(BF16), state, 1, 1)

    @pl.when(g == 0)
    def _():
        acc_ref[...] = gm1_ref[...]

    acc_ref[:, :STATE] += d_in
    acc_ref[:, STATE:] += d_out

    @pl.when(g == pl.num_programs(1) - 1)
    def _():
        dx_ref[:, dx_ref.shape[1] - 2 * STATE :] = acc_ref[...].astype(BF16)


def params(order):
    return pltpu.CompilerParams(vmem_limit_bytes=VMEM_LIMIT, dimension_semantics=order)


def shifted(value, axis, by):
    peers = lax.axis_size(axis)
    pairs = [(i, i + by) for i in range(peers) if 0 <= i + by < peers]
    return lax.ppermute(value, axis, pairs)


def local(conv_input, conv_weight, conv_bias, step_size, log_decay, skip_gain, grad_output):
    taps_count = conv_weight.shape[0]
    tok_rows, channels = conv_input.shape
    heads_here, seq_rows = step_size.shape
    lanes = grad_output.shape[1]
    head_dim = lanes // heads_here
    peers = lax.axis_size("head")
    ctx = lax.axis_size("ctx")
    blocks = seq_rows // BLOCK
    groups = heads_here // GROUP
    width = GROUP * head_dim
    inner = peers * lanes
    full = lanes + 2 * STATE
    map_at = lanes // (2 * STATE)

    earlier = shifted(conv_input[tok_rows - (taps_count - 1) :], ("ctx", "head"), 1)
    padded = jnp.concatenate([earlier, conv_input], axis=0).astype(F32)
    preact = conv_bias[None, :] + conv_weight[0][None, :] * padded[0:tok_rows]
    for offset in range(1, taps_count):
        preact = preact + conv_weight[offset][None, :] * padded[offset : offset + tok_rows]
    activated, silu_back = jax.vjp(jax.nn.silu, preact)
    activated = activated.astype(BF16)
    maps = activated[:, inner:]
    send = jnp.concatenate(
        [
            jnp.concatenate([activated[:, i * lanes : (i + 1) * lanes], maps], axis=1)
            for i in range(peers)
        ],
        axis=0,
    )
    got = lax.all_to_all(send, "head", split_axis=0, concat_axis=0, tiled=True)

    part = lanes // ctx
    pieces = ctx // groups
    gb = [
        pl.BlockSpec((BLOCK, width), lambda g, b: (b, g)),
        pl.BlockSpec((BLOCK, 2 * STATE), lambda g, b: (b, map_at)),
        pl.BlockSpec((BLOCK, width), lambda g, b: (b, g)),
        pl.BlockSpec((GROUP, BLOCK), lambda g, b: (g, b)),
        pl.BlockSpec((GROUP, BLOCK), lambda g, b: (g, b)),
    ]
    bg = [
        pl.BlockSpec((BLOCK, width), lambda b, g: (b, g)),
        pl.BlockSpec((BLOCK, 2 * STATE), lambda b, g: (b, map_at)),
        pl.BlockSpec((BLOCK, width), lambda b, g: (b, g)),
        pl.BlockSpec((GROUP, BLOCK), lambda b, g: (g, b)),
        pl.BlockSpec((GROUP, BLOCK), lambda b, g: (g, b)),
    ]
    tile = pl.BlockSpec((BLOCK, width), lambda b, g: (b, g))
    rows = pl.BlockSpec((GROUP, BLOCK), lambda b, g: (g, b))
    mapgrad = pl.BlockSpec((BLOCK, 2 * STATE), lambda b, g: (b, 0))

    inc, gp, dec, packed = pl.pallas_call(
        partial(states_kernel, head_dim),
        grid=(groups, blocks),
        in_specs=gb,
        out_specs=[
            pl.BlockSpec((1, STATE, width), lambda g, b: (b, 0, g)),
            pl.BlockSpec((1, STATE, width), lambda g, b: (b, 0, g)),
            pl.BlockSpec((1, GROUP, width), lambda g, b: (b, 0, g)),
            pl.BlockSpec((pieces, 2 * STATE + 2 * GROUP, part), lambda g, b: (g, 0, 0)),
        ],
        out_shape=[
            jax.ShapeDtypeStruct((blocks, STATE, lanes), F32),
            jax.ShapeDtypeStruct((blocks, STATE, lanes), F32),
            jax.ShapeDtypeStruct((blocks, GROUP, lanes), F32),
            jax.ShapeDtypeStruct((ctx, 2 * STATE + 2 * GROUP, part), BF16),
        ],
        scratch_shapes=[
            pltpu.VMEM((STATE, width), F32),
            pltpu.VMEM((STATE, width), F32),
            pltpu.VMEM((GROUP, width), F32),
        ],
        compiler_params=params(("arbitrary", "arbitrary")),
        name="states",
    )(got, got, grad_output, log_decay, step_size)

    mine = lax.all_to_all(packed, "ctx", split_axis=0, concat_axis=0, tiled=True)
    chained = pl.pallas_call(
        chain_kernel,
        out_shape=jax.ShapeDtypeStruct((ctx, 2 * STATE, part), BF16),
        compiler_params=pltpu.CompilerParams(vmem_limit_bytes=VMEM_LIMIT),
        name="chain",
    )(mine)
    entering = lax.all_to_all(chained, "ctx", split_axis=0, concat_axis=0, tiled=True)

    skip = jnp.broadcast_to(jnp.repeat(skip_gain, head_dim)[None, :], (GROUP, lanes))
    y1, dx1, gs1, gc1, gm1 = pl.pallas_call(
        partial(intra_kernel, head_dim),
        grid=(blocks, groups),
        in_specs=bg + [pl.BlockSpec((GROUP, width), lambda b, g: (0, g))],
        out_specs=[tile, tile, rows, rows, mapgrad],
        out_shape=[
            jax.ShapeDtypeStruct((seq_rows, lanes), BF16),
            jax.ShapeDtypeStruct((seq_rows, lanes), BF16),
            jax.ShapeDtypeStruct((heads_here, seq_rows), F32),
            jax.ShapeDtypeStruct((heads_here, seq_rows), F32),
            jax.ShapeDtypeStruct((seq_rows, 2 * STATE), F32),
        ],
        scratch_shapes=[pltpu.VMEM((BLOCK, BLOCK), F32), pltpu.VMEM((BLOCK, BLOCK), F32)],
        compiler_params=params(("arbitrary", "arbitrary")),
        cost_estimate=pl.CostEstimate(
            flops=20_000_000_000, bytes_accessed=20_000_000, transcendentals=6_000_000
        ),
        name="intra",
    )(got, got, grad_output, log_decay, step_size, skip)

    def once(*shape):
        return pl.BlockSpec(shape, lambda b, g: (0, 0, jnp.where(b == 0, g, groups - 1)))

    y, dx, grad_steps, grad_rates = pl.pallas_call(
        partial(carry_kernel, head_dim),
        grid=(blocks, groups),
        in_specs=bg
        + [
            tile,
            tile,
            rows,
            rows,
            mapgrad,
            once(blocks, STATE, width),
            once(blocks, STATE, width),
            once(blocks, GROUP, width),
            pl.BlockSpec((pieces, 2 * STATE, part), lambda b, g: (jnp.where(b == 0, g, groups - 1), 0, 0)),
        ],
        out_specs=[tile, pl.BlockSpec((BLOCK, full), lambda b, g: (b, 0)), rows, rows],
        out_shape=[
            jax.ShapeDtypeStruct((seq_rows, lanes), BF16),
            jax.ShapeDtypeStruct((seq_rows, full), BF16),
            jax.ShapeDtypeStruct((heads_here, seq_rows), F32),
            jax.ShapeDtypeStruct((heads_here, seq_rows), F32),
        ],
        scratch_shapes=[
            pltpu.VMEM((blocks, groups, STATE, width), BF16),
            pltpu.VMEM((blocks, groups, STATE, width), BF16),
            pltpu.VMEM((blocks, groups, GROUP, 128), F32),
            pltpu.VMEM((BLOCK, 2 * STATE), F32),
        ],
        compiler_params=params(("arbitrary", "arbitrary")),
        name="carry",
    )(got, got, grad_output, log_decay, step_size, y1, dx1, gs1, gc1, gm1, inc, gp, dec, entering)

    back = lax.all_to_all(dx, "head", split_axis=0, concat_axis=0, tiled=True)
    back = back.reshape(peers, tok_rows, full)
    map_grads = jnp.sum(back[:, :, lanes:].astype(F32), axis=0).astype(BF16)
    grad_act = jnp.concatenate([back[i, :, :lanes] for i in range(peers)] + [map_grads], axis=1)
    grad_pre = silu_back(grad_act.astype(F32))[0]
    following = shifted(grad_pre[: taps_count - 1], ("ctx", "head"), -1)
    extended = jnp.concatenate([grad_pre, following], axis=0)
    total = conv_weight[taps_count - 1][None, :] * extended[0:tok_rows]
    for offset in range(taps_count - 2, -1, -1):
        begin = taps_count - 1 - offset
        total = total + conv_weight[offset][None, :] * extended[begin : begin + tok_rows]
    return (y, total.astype(BF16), grad_steps, grad_rates)


def solution(mesh):
    return jax.shard_map(
        local,
        mesh=mesh,
        in_specs=(
            P(("ctx", "head"), None),
            P(),
            P(),
            P("head", "ctx"),
            P("head", "ctx"),
            P("head"),
            P("ctx", "head"),
        ),
        out_specs=(P("ctx", "head"), P(("ctx", "head"), None), P("head", "ctx"), P("head", "ctx")),
        check_vma=False,
    )
```

time: 909 us -> 239 us (0.26); the launches traced: 897 us -> 237 us
  waiting for transfers between devices: 357 us -> 28.2 us
  local copies, waits for them, and re-layouts: 225 us -> 3.32 us
  matrix products: 119 us -> 0 us
  other arithmetic: 114 us -> 17.9 us
  blocking collectives: 6.58 us -> 91.6 us
  Pallas kernels: 0 us -> 77.6 us
  starting transfers between devices: 58.9 us -> 17.2 us
  between operations: 14.8 us -> 0.84 us
    ppermute x16 -> x2, waiting for transfers between devices: 311 us -> 3.38 us  [shifted(): return lax.ppermute(value, axis, pairs)]
    dot_general x43 -> x0, matrix products: 119 us -> none  [the longest x9 50.8 us: block_update(): jnp.einsum('hts,shp->thp', weights, features, preferred_element_type=jnp....]
    all_to_all x0 -> x2, blocking collectives: none -> 91.6 us  [the longest x1 46.3 us: local(): got = lax.all_to_all(send, 'head', split_axis=0, concat_axis=0, tiled=True)]
    pallas_call x0 -> x4, Pallas kernels: none -> 77.6 us  [the longest x1 32.8 us: local(): pl.pallas_call(partial(intra_kernel, head_dim), grid=(blocks, groups), in...]
    ppermute x16 -> x2, starting transfers between devices: 49.6 us -> 6.63 us  [shifted(): return lax.ppermute(value, axis, pairs)]
    dynamic_slice x36 -> x0, local copies, waits for them, and re-layouts: 38.9 us -> none  [the longest x6 17.5 us: sequence_ssd(): lax.scan(update, entering, (feats_b, steps_b, input_b, output_b, rates_b))]
    unnamed x40 -> x16, local copies, waits for them, and re-layouts: 35.3 us -> 0.24 us
    reduce_scatter x1 -> x0, waiting for transfers between devices: 29.7 us -> none  [local(): lax.psum_scatter(jnp.concatenate([grad_inmap, grad_outmap], axis=1), 'hea...]
  transfers between devices with their start and end apart: 19 -> 4, of which waited for: 17 -> 2; matrix products, arithmetic and copies ran while one was open for 8% -> 1% of each run, Pallas kernels for 0% -> 14%
where the time goes in v1:
time: 239 us; the launch traced here: 237 us
  blocking collectives  91.6 us (38%)
  Pallas kernels  77.6 us (32%)
  waiting for transfers between devices  28.2 us (12%)
  other arithmetic  17.9 us (7%)
  starting transfers between devices  17.2 us (7%)
  local copies, waits for them, and re-layouts  3.32 us (1%)
    all_to_all x1, blocking collectives, local(): got = lax.all_to_all(send, 'head', split_axis=0, concat_axis=0, tiled=True)  46.3 us
    all_to_all x1, blocking collectives, local(): back = lax.all_to_all(dx, 'head', split_axis=0, concat_axis=0, tiled=True)  45.3 us
    pallas_call x1, Pallas kernels, local(): pl.pallas_call(partial(intra_kernel, head_dim), grid=(blocks, groups), in...  32.8 us
    pallas_call x1, Pallas kernels, local(): pl.pallas_call(partial(carry_kernel, head_dim), grid=(blocks, groups), in...  27.8 us
    all_to_all x1, waiting for transfers between devices, local(): lax.all_to_all(packed, 'ctx', split_axis=0, concat_axis=0, tiled=True)  24.9 us
    pallas_call x1, Pallas kernels, local(): pl.pallas_call(partial(states_kernel, head_dim), grid=(groups, blocks), i...  15.7 us
    ppermute x2, starting transfers between devices, shifted(): return lax.ppermute(value, axis, pairs)  6.63 us
    all_to_all x1, starting transfers between devices, local(): lax.all_to_all(chained, 'ctx', split_axis=0, concat_axis=0, tiled=True)  5.94 us
  transfers between devices with their start and end apart: 4, of which 2 were waited for; matrix products, arithmetic and copies ran while one was open for 1% of the time, Pallas kernels for 14%

profile of v1, /device:TPU:25, one launch (start us, length us, event | category | flops | bytes accessed | tf_op | source)
XLA Modules:
  0.0 236.6 jit_solution(1170240194739355945)
XLA Ops:
  0.6 0.0 copy-start.2
  0.6 1.0 slice.73
  1.6 3.7 %collective-permute-start = (bf16[3,8448]{1,0:T(4,128)(2,1)S(1)}, bf16[3,8448]{1,0:T(4,128)(2,1)S(1)}, u32[]{:S(2)}, u32[]{:S(2)}) collective-permute-start(bf16[3,8448]{1,0:T(4,128)(2,1)S(1)} %slice.73), channel_id=1, source_target_pairs={{0,1},{1,2},{2,3},{3,4},{4,5},{5,6},{6,7},{7,8},{8,9},{9,10},{10,1... | collective-permute-start | bytes 152072 | tf_op jit(solution)/shard_map/ppermute | solution.py:236
  5.3 1.6 slice_reduce_fusion.4
  6.9 0.0 collective-permute-done
  6.9 2.6 %maximum_convert_fusion = f32[195,8448]{1,0:T(8,128)S(1)} fusion(bf16[192,8448]{1,0:T(8,128)(2,1)} %param.7, bf16[3,8448]{1,0:T(4,128)(2,1)S(1)} %collective-permute-done), kind=kLoop, calls=%fused_computation.30 | loop fusion | flops 6589440 | bytes 9884160 | tf_op jit(solution)/shard_map/convert_element_type | solution.py:255
  9.5 0.0 copy-done.2
  9.5 5.5 %multiply_convert_fusion = (bf16[192,8448]{1,0:T(8,128)(2,1)S(1)}, f32[192,8448]{1,0:T(8,128)}) fusion(f32[195,8448]{1,0:T(8,128)S(1)} %maximum_convert_fusion, f32[8448]{0:T(1024)S(1)} %get-tuple-element.32, f32[8448]{0:T(1024)S(1)} %get-tuple-element.33, f32[8448]{0:T(1024)S(1)} %get-tuple-element.31, f32[8448]{0:T(1024)S(1)} %get-tuple-element.30, ...), kind=kLoop, calls=%fused_computation.27 | loop fusion | flops 21086208 | bytes 35853312 | tf_op jit(solution)/shard_map/convert_element_type | solution.py:260
  15.0 0.1 concatenate.32
  15.1 0.3 fusion.20
  15.4 0.0 copy-start
  15.4 0.0 copy-start.1
  15.4 2.6 %pad_maximum_fusion.1 = bf16[768,2304]{1,0:T(8,128)(2,1)S(1)} fusion(bf16[192,2304]{1,0:T(8,128)(2,1)S(1)} %concatenate.32, bf16[192,256]{1,0:T(8,128)(2,1)S(1)} %slice.99, bf16[192,2048]{1,0:T(8,128)(2,1)S(1)} %get-tuple-element.37, bf16[192,2048]{1,0:T(8,128)(2,1)S(1)} %get-tuple-element.38, bf16[192,2048]{1,0:T(8,128)(2,1)S(1)} %get-tuple-element.36), kind=kLoop, calls=%fused_computation.29 | loop fusion | flops 24772608 | bytes 6881280 | tf_op jit(solution)/shard_map/concatenate | solution.py:262
  18.0 46.3 %all_to_all.30 = bf16[4,192,2304]{2,1,0:T(8,128)(2,1)} all-to-all(bf16[4,192,2304]{2,1,0:T(8,128)(2,1)S(1)} %bitcast.27), channel_id=1, replica_groups=mesh['ctx'=8,'head'=4] {'head'}, dimensions={0} | all-to-all | bytes 7077888 | tf_op jit(solution)/shard_map/all_to_all | solution.py:269
  64.3 0.0 copy-start.3
  64.3 0.0 copy-done
  64.3 0.0 copy-done.1
  64.3 15.7 %states.1 = (f32[3,128,2048]{2,1,0:T(8,128)}, f32[3,128,2048]{2,1,0:T(8,128)}, f32[3,8,2048]{2,1,0:T(8,128)S(1)}, bf16[8,272,256]{2,1,0:T(8,128)(2,1)}) custom-call(bf16[768,2304]{1,0:T(8,128)(2,1)} %bitcast.19, bf16[768,2304]{1,0:T(8,128)(2,1)} %bitcast.20, bf16[768,2048]{1,0:T(8,128)(2,1)} %dy_ref.5, f32[32,768]{1,0:T(8,128)S(1)} %copy-done, ...), custom_call_target="tpu_custom_call" | custom-call | tf_op jit(solution)/shard_map/states/pallas_call | solution.py:291
  80.0 4.6 %all-to-all-start.1 = ((bf16[8,272,256]{2,1,0:T(8,128)(2,1)}), bf16[8,272,256]{2,1,0:T(8,128)(2,1)S(1)}, u32[]{:S(2)}, u32[]{:S(2)}) async-start(bf16[8,272,256]{2,1,0:T(8,128)(2,1)} %get-tuple-element.25), calls=%async_computation.1 | async-start | bytes 2228224 | tf_op jit(solution)/shard_map/all_to_all | solution.py:316
  84.6 0.0 copy-done.3
  84.6 0.1 broadcast_in_dim.11
  84.7 0.1 broadcast_in_dim.12
  84.8 24.9 %all-to-all-done.1.in_ref = bf16[8,272,256]{2,1,0:T(8,128)(2,1)S(1)} async-done(((bf16[8,272,256]{2,1,0:T(8,128)(2,1)}), bf16[8,272,256]{2,1,0:T(8,128)(2,1)S(1)}, u32[]{:S(2)}, u32[]{:S(2)}) %all-to-all-start.1) | async-done | bytes 1114144 | tf_op jit(solution)/shard_map/all_to_all | solution.py:316
  109.6 1.2 chain.1
  110.8 5.9 %all-to-all-start.2 = ((bf16[8,256,256]{2,1,0:T(8,128)(2,1)}), bf16[8,256,256]{2,1,0:T(8,128)(2,1)S(1)}, u32[]{:S(2)}, u32[]{:S(2)}) async-start(bf16[8,256,256]{2,1,0:T(8,128)(2,1)} %chain.1), calls=%async_computation.2 | async-start | bytes 2097152 | tf_op jit(solution)/shard_map/all_to_all | solution.py:323
  116.8 32.8 %intra.1 = (bf16[768,2048]{1,0:T(8,128)(2,1)}, bf16[768,2048]{1,0:T(8,128)(2,1)}, f32[32,768]{1,0:T(8,128)S(1)}, f32[32,768]{1,0:T(8,128)S(1)}, f32[768,256]{1,0:T(8,128)S(1)}) custom-call(bf16[768,2304]{1,0:T(8,128)(2,1)} %bitcast.21, bf16[768,2304]{1,0:T(8,128)(2,1)} %bitcast.22, bf16[768,2048]{1,0:T(8,128)(2,1)} %dy_ref.5, f32[32,768]{1,0:T(8,128)S(1)} %copy-done, ...), custom_call_target="tpu_custom_call" | custom-call | flops 20000000000 | bytes 20000000 | tf_op jit(solution)/shard_map/intra/pallas_call | solution.py:326
  149.6 0.0 all-to-all-done.2.enter_ref
  149.6 27.8 %carry.1 = (bf16[768,2048]{1,0:T(8,128)(2,1)}, bf16[768,2304]{1,0:T(8,128)(2,1)}, f32[32,768]{1,0:T(8,128)}, f32[32,768]{1,0:T(8,128)}) custom-call(bf16[768,2304]{1,0:T(8,128)(2,1)} %bitcast.23, bf16[768,2304]{1,0:T(8,128)(2,1)} %bitcast.24, bf16[768,2048]{1,0:T(8,128)(2,1)} %dy_ref.5, f32[32,768]{1,0:T(8,128)S(1)} %copy-done, f32[32,768]{1,0:T(8,128)S(1)} %copy-done.1, ...), custom_call_target="tpu_custom_call" | custom-call | tf_op jit(solution)/shard_map/carry/pallas_call | solution.py:349
  177.4 0.0 slice-start
  177.5 0.0 slice-start.1
  177.5 45.3 %all_to_all.31 = bf16[4,192,2304]{2,1,0:T(8,128)(2,1)S(1)} all-to-all(bf16[4,192,2304]{2,1,0:T(8,128)(2,1)} %bitcast.28), channel_id=1, replica_groups=mesh['ctx'=8,'head'=4] {'head'}, dimensions={0} | all-to-all | bytes 7077888 | tf_op jit(solution)/shard_map/all_to_all | solution.py:381
  222.8 0.1 slice_reduce_fusion
  222.8 0.1 fusion.18
  222.9 0.1 fusion.17
  223.0 0.1 fusion.16
  223.0 0.1 fusion.15
  223.1 0.0 slice-done
  223.1 0.0 slice-done.1
  223.1 2.4 %fusion.8 = f32[192,8448]{1,0:T(8,128)S(1)} fusion(bf16[192,8448]{1,0:T(8,128)(2,1)S(1)} %constant_dynamic-update-slice_fusion, f32[192,8448]{1,0:T(8,128)S(1)} %bitcast.26), kind=kLoop, calls=%fused_computation.15 | loop fusion | flops 16220160 | bytes 16220160 | tf_op jit(solution)/shard_map/transpose(jvp(jit(silu)))/add_any | solution.py:259
  225.6 2.9 %collective-permute-start.1 = (f32[3,8448]{1,0:T(4,128)S(1)}, f32[3,8448]{1,0:T(4,128)S(1)}, u32[]{:S(2)}, u32[]{:S(2)}) collective-permute-start(f32[3,8448]{1,0:T(4,128)S(1)} %slice.107), channel_id=1, source_target_pairs={{1,0},{2,1},{3,2},{4,3},{5,4},{6,5},{7,6},{8,7},{9,8},{10,9},{11,1... | collective-permute-start | bytes 304136 | tf_op jit(solution)/shard_map/ppermute | solution.py:236
  228.5 3.4 %collective-permute-done.1 = f32[3,8448]{1,0:T(4,128)S(1)} collective-permute-done((f32[3,8448]{1,0:T(4,128)S(1)}, f32[3,8448]{1,0:T(4,128)S(1)}, u32[]{:S(2)}, u32[]{:S(2)}) %collective-permute-start.1) | collective-permute-done | bytes 101408 | tf_op jit(solution)/shard_map/ppermute | solution.py:236
  231.9 4.7 %fusion.4 = bf16[192,8448]{1,0:T(8,128)(2,1)} fusion(f32[192,8448]{1,0:T(8,128)S(1)} %fusion.8, f32[3,8448]{1,0:T(4,128)S(1)} %collective-permute-done.1, f32[8448]{0:T(1024)S(1)} %get-tuple-element.32, f32[8448]{0:T(1024)S(1)} %get-tuple-element.33, f32[8448]{0:T(1024)S(1)} %get-tuple-element.31, f32[8448]{0:T(1024)S(1)} %get-tuple-element.30), kind=kLoop, calls=%fused_computation.11 | loop fusion | flops 17842176 | bytes 9968640 | tf_op jit(solution)/shard_map/convert_element_type | solution.py:392
  (5 shorter events, 0.0 us)
Async XLA Ops:
  0.6 8.8 %copy-start.2 = (f32[8448]{0:T(1024)S(1)}, f32[8448]{0:T(1024)}, u32[]{:S(2)}) copy-start(f32[8448]{0:T(1024)} %param.9) | copy-start | bytes 101380
  1.6 5.3 %collective-permute-start = (bf16[3,8448]{1,0:T(4,128)(2,1)S(1)}, bf16[3,8448]{1,0:T(4,128)(2,1)S(1)}, u32[]{:S(2)}, u32[]{:S(2)}) collective-permute-start(bf16[3,8448]{1,0:T(4,128)(2,1)S(1)} %slice.73), channel_id=1, source_target_pairs={{0,1},{1,2},{2,3},{3,4},{4,5},{5,6},{6,7},{7,8},{8,9},{9,10},{10,1... | collective-permute-start | bytes 152072 | tf_op jit(solution)/shard_map/ppermute | solution.py:236
  15.4 48.9 %copy-start = (f32[32,768]{1,0:T(8,128)S(1)}, f32[32,768]{1,0:T(8,128)}, u32[]{:S(2)}) copy-start(f32[32,768]{1,0:T(8,128)} %rate_ref.5) | copy-start | bytes 294916
  15.4 48.9 %copy-start.1 = (f32[32,768]{1,0:T(8,128)S(1)}, f32[32,768]{1,0:T(8,128)}, u32[]{:S(2)}) copy-start(f32[32,768]{1,0:T(8,128)} %step_ref.5) | copy-start | bytes 294916
  64.3 20.3 %copy-start.3 = (f32[32]{0:T(128)S(1)}, f32[32]{0:T(128)}, u32[]{:S(2)}) copy-start(f32[32]{0:T(128)} %param.12) | copy-start | bytes 388
  80.0 29.6 %all-to-all-start.1 = ((bf16[8,272,256]{2,1,0:T(8,128)(2,1)}), bf16[8,272,256]{2,1,0:T(8,128)(2,1)S(1)}, u32[]{:S(2)}, u32[]{:S(2)}) async-start(bf16[8,272,256]{2,1,0:T(8,128)(2,1)} %get-tuple-element.25), calls=%async_computation.1 | async-start | bytes 2228224 | tf_op jit(solution)/shard_map/all_to_all | solution.py:316
  110.8 38.8 %all-to-all-start.2 = ((bf16[8,256,256]{2,1,0:T(8,128)(2,1)}), bf16[8,256,256]{2,1,0:T(8,128)(2,1)S(1)}, u32[]{:S(2)}, u32[]{:S(2)}) async-start(bf16[8,256,256]{2,1,0:T(8,128)(2,1)} %chain.1), calls=%async_computation.2 | async-start | bytes 2097152 | tf_op jit(solution)/shard_map/all_to_all | solution.py:323
  177.4 45.7 %slice-start = ((s8[6488064]{0:T(1024)(128)(4,1)}), s8[4194304]{0:T(1024)(128)(4,1)S(1)}, s32[]{:S(2)}) async-start(s8[6488064]{0:T(1024)(128)(4,1)} %bitcast.25), calls=%async_computation.4 | async-start | bytes 8388608
  177.5 45.7 %slice-start.1 = ((s8[6488064]{0:T(1024)(128)(4,1)}), s8[2293760]{0:T(1024)(128)(4,1)S(1)}, s32[]{:S(2)}) async-start(s8[6488064]{0:T(1024)(128)(4,1)} %bitcast.25), calls=%async_computation.5 | async-start | bytes 4587520
  225.6 6.3 %collective-permute-start.1 = (f32[3,8448]{1,0:T(4,128)S(1)}, f32[3,8448]{1,0:T(4,128)S(1)}, u32[]{:S(2)}, u32[]{:S(2)}) collective-permute-start(f32[3,8448]{1,0:T(4,128)S(1)} %slice.107), channel_id=1, source_target_pairs={{1,0},{2,1},{3,2},{4,3},{5,4},{6,5},{7,6},{8,7},{9,8},{10,9},{11,1... | collective-permute-start | bytes 304136 | tf_op jit(solution)/shard_map/ppermute | solution.py:236

commit v2 on v1

--- a/solution.py
+++ b/solution.py
@@ -9,15 +9,15 @@
 
 STATE = 128
 BLOCK = 256
-GROUP = 8
+GROUP = 16
 F32 = jnp.float32
 BF16 = jnp.bfloat16
 VMEM_LIMIT = 50 * 1024 * 1024
 
 
-def dot(a, b, ca, cb, precision=None):
+def dot(a, b, ca, cb):
     return lax.dot_general(
-        a, b, (((ca,), (cb,)), ((), ())), precision=precision, preferred_element_type=F32
+        a, b, (((ca,), (cb,)), ((), ())), preferred_element_type=F32
     )
 
 
@@ -47,11 +47,20 @@
 def earlier_or_same(length):
     row = lax.broadcasted_iota(jnp.int32, (length, length), 0)
     col = lax.broadcasted_iota(jnp.int32, (length, length), 1)
-    return jnp.where(row <= col, 1.0, 0.0)
+    return jnp.where(row <= col, 1.0, 0.0).astype(BF16)
+
+
+def triangular(rows, contract):
+    high = rows.astype(BF16).astype(F32)
+    rest = rows - high
+    middle = rest.astype(BF16).astype(F32)
+    terms = jnp.concatenate([high, middle, rest - middle, jnp.zeros_like(rows)], axis=0)
+    sums = dot(terms.astype(BF16), earlier_or_same(rows.shape[1]), 1, contract)
+    return sums[:GROUP] + sums[GROUP : 2 * GROUP] + sums[2 * GROUP : 3 * GROUP]
 
 
 def running_sum(rates):
-    return dot(rates, earlier_or_same(rates.shape[1]), 1, 0, lax.Precision.HIGHEST)
+    return triangular(rates, 0)
 
 
 def states_kernel(head_dim, x_ref, m_ref, dy_ref, rate_ref, step_ref, inc_ref, gp_ref, dec_ref, pack_ref, t_ref, r_ref, d_ref):
@@ -113,7 +122,8 @@
         grad = decay(c) * grad + in_ref[c, STATE : 2 * STATE].astype(F32)
 
 
-def intra_kernel(head_dim, x_ref, m_ref, dy_ref, rate_ref, step_ref, skip_ref, y_ref, dx_ref, gs_ref, gc_ref, gm_ref, aff_ref, da_ref):
+def intra_kernel(head_dim, x_ref, m_ref, dy_ref, rate_ref, step_ref, skip_ref, *refs):
+    y_ref, dx_ref, gs_ref, gc_ref, gm_ref, aff_ref, da_ref = refs[-7:]
     g = pl.program_id(1)
     width = x_ref.shape[1]
     row = lax.broadcasted_iota(jnp.int32, (BLOCK, BLOCK), 0)
@@ -167,7 +177,8 @@
 
 
 def carry_kernel(head_dim, x_ref, m_ref, dy_ref, rate_ref, step_ref, y1_ref, dx1_ref, gs1_ref, gc1_ref, gm1_ref,
-                 inc_ref, gp_ref, dec_ref, enter_ref, y_ref, dx_ref, gs_ref, gd_ref, s_ref, g_ref, dot_ref, acc_ref):
+                 inc_ref, gp_ref, dec_ref, enter_ref, *refs):
+    y_ref, dx_ref, gs_ref, gd_ref, s_ref, g_ref, dot_ref, acc_ref = refs[-8:]
     b, g = pl.program_id(0), pl.program_id(1)
     width = x_ref.shape[1]
     blocks = inc_ref.shape[0]
@@ -210,13 +221,15 @@
     gc = gc1_ref[...] + head_sums(dy * carried, head_dim) - weight * xq
     at = lax.broadcasted_iota(jnp.int32, gc.shape, 1)
     gc = gc + jnp.where(at == BLOCK - 1, dot_ref[b, g][:, 0:1], 0.0)
-    gd_ref[...] = dot(gc, earlier_or_same(BLOCK), 1, 1, lax.Precision.HIGHEST)
+    gd_ref[...] = triangular(gc, 1)
     d_in = dot((x * to_end).astype(BF16), grad, 1, 1)
     d_out = dot((dy * from_start).astype(BF16), state, 1, 1)
 
     @pl.when(g == 0)
     def _():
         acc_ref[...] = gm1_ref[...]
+        for more_ref in refs[:-8]:
+            acc_ref[...] += more_ref[...]
 
     acc_ref[:, :STATE] += d_in
     acc_ref[:, STATE:] += d_out
@@ -313,35 +326,63 @@
         name="states",
     )(got, got, grad_output, log_decay, step_size)
 
-    mine = lax.all_to_all(packed, "ctx", split_axis=0, concat_axis=0, tiled=True)
-    chained = pl.pallas_call(
-        chain_kernel,
-        out_shape=jax.ShapeDtypeStruct((ctx, 2 * STATE, part), BF16),
-        compiler_params=pltpu.CompilerParams(vmem_limit_bytes=VMEM_LIMIT),
-        name="chain",
-    )(mine)
-    entering = lax.all_to_all(chained, "ctx", split_axis=0, concat_axis=0, tiled=True)
+    def columns(value):
+        return lax.all_to_all(value, "ctx", split_axis=0, concat_axis=0, tiled=True)
+
+    def chain(mine):
+        return pl.pallas_call(
+            chain_kernel,
+            out_shape=jax.ShapeDtypeStruct((ctx, 2 * STATE, part), BF16),
+            compiler_params=pltpu.CompilerParams(vmem_limit_bytes=VMEM_LIMIT),
+            name="chain",
+        )(mine)
+
+    mine = columns(packed)
 
     skip = jnp.broadcast_to(jnp.repeat(skip_gain, head_dim)[None, :], (GROUP, lanes))
-    y1, dx1, gs1, gc1, gm1 = pl.pallas_call(
-        partial(intra_kernel, head_dim),
-        grid=(blocks, groups),
-        in_specs=bg + [pl.BlockSpec((GROUP, width), lambda b, g: (0, g))],
-        out_specs=[tile, tile, rows, rows, mapgrad],
-        out_shape=[
-            jax.ShapeDtypeStruct((seq_rows, lanes), BF16),
-            jax.ShapeDtypeStruct((seq_rows, lanes), BF16),
-            jax.ShapeDtypeStruct((heads_here, seq_rows), F32),
-            jax.ShapeDtypeStruct((heads_here, seq_rows), F32),
-            jax.ShapeDtypeStruct((seq_rows, 2 * STATE), F32),
-        ],
-        scratch_shapes=[pltpu.VMEM((BLOCK, BLOCK), F32), pltpu.VMEM((BLOCK, BLOCK), F32)],
-        compiler_params=params(("arbitrary", "arbitrary")),
-        cost_estimate=pl.CostEstimate(
-            flops=20_000_000_000, bytes_accessed=20_000_000, transcendentals=6_000_000
-        ),
-        name="intra",
-    )(got, got, grad_output, log_decay, step_size, skip)
+    SHARES = 2 if groups % 2 == 0 else 1
+    share = groups // SHARES
+
+    def intra(k, before):
+        at = k * share
+        wide = pl.BlockSpec((BLOCK, width), lambda b, g: (b, g + at))
+        thin = pl.BlockSpec((GROUP, BLOCK), lambda b, g: (g + at, b))
+        return pl.pallas_call(
+            partial(intra_kernel, head_dim),
+            grid=(blocks, share),
+            in_specs=[
+                wide,
+                bg[1],
+                wide,
+                thin,
+                thin,
+                pl.BlockSpec((GROUP, width), lambda b, g: (0, g + at)),
+            ]
+            + [pl.BlockSpec(memory_space=pl.ANY)] * len(before),
+            out_specs=[wide, wide, thin, thin, mapgrad],
+            out_shape=[
+                jax.ShapeDtypeStruct((seq_rows, lanes), BF16),
+                jax.ShapeDtypeStruct((seq_rows, lanes), BF16),
+                jax.ShapeDtypeStruct((heads_here, seq_rows), F32),
+                jax.ShapeDtypeStruct((heads_here, seq_rows), F32),
+                jax.ShapeDtypeStruct((seq_rows, 2 * STATE), F32),
+            ],
+            scratch_shapes=[pltpu.VMEM((BLOCK, BLOCK), F32), pltpu.VMEM((BLOCK, BLOCK), F32)],
+            compiler_params=params(("arbitrary", "arbitrary")),
+            cost_estimate=pl.CostEstimate(
+                flops=10_000_000_000, bytes_accessed=50_000_000, transcendentals=3_000_000
+            ),
+            input_output_aliases={6 + i: i for i in range(len(before))},
+            name="intra",
+        )(got, got, grad_output, log_decay, step_size, skip, *before)
+
+    *first, gm1 = intra(0, [])
+    mine, first[2] = lax.optimization_barrier((mine, first[2]))
+    entering = columns(chain(mine))
+    gm2 = []
+    if SHARES == 2:
+        *first, more = intra(1, first)
+        gm2 = [more]
 
     def once(*shape):
         return pl.BlockSpec(shape, lambda b, g: (0, 0, jnp.where(b == 0, g, groups - 1)))
@@ -360,7 +401,8 @@
             once(blocks, STATE, width),
             once(blocks, GROUP, width),
             pl.BlockSpec((pieces, 2 * STATE, part), lambda b, g: (jnp.where(b == 0, g, groups - 1), 0, 0)),
-        ],
+        ]
+        + [mapgrad] * len(gm2),
         out_specs=[tile, pl.BlockSpec((BLOCK, full), lambda b, g: (b, 0)), rows, rows],
         out_shape=[
             jax.ShapeDtypeStruct((seq_rows, lanes), BF16),
@@ -376,7 +418,7 @@
         ],
         compiler_params=params(("arbitrary", "arbitrary")),
         name="carry",
-    )(got, got, grad_output, log_decay, step_size, y1, dx1, gs1, gc1, gm1, inc, gp, dec, entering)
+    )(got, got, grad_output, log_decay, step_size, *first, gm1, inc, gp, dec, entering, *gm2)
 
     back = lax.all_to_all(dx, "head", split_axis=0, concat_axis=0, tiled=True)
     back = back.reshape(peers, tok_rows, full)

time: 239 us -> 220 us (0.921)
  Pallas kernels: 77.6 us -> 59.8 us
  waiting for transfers between devices: 28.2 us -> 22 us
  local copies, waits for them, and re-layouts: 3.32 us -> 7.32 us
    pallas_call x1, Pallas kernels: 27.8 us -> 20.2 us  [local(): pl.pallas_call(partial(carry_kernel, head_dim), grid=(blocks, groups), in...]
    all_to_all x2, waiting for transfers between devices: 24.9 us -> 18.6 us  [columns(): return lax.all_to_all(value, 'ctx', split_axis=0, concat_axis=0, tiled=True)]
    pallas_call x1, Pallas kernels: 15.7 us -> 9.98 us  [local(): pl.pallas_call(partial(states_kernel, head_dim), grid=(groups, blocks), i...]
    pallas_call x2 -> x3, Pallas kernels: 34 us -> 29.7 us  [the longest x2 28.5 us: intra(): pl.pallas_call(partial(intra_kernel, head_dim), grid=(blocks, share), in_...]
    unnamed x16 -> x36, local copies, waits for them, and re-layouts: 0.24 us -> 4.22 us
  transfers between devices with their start and end apart: 4 -> 4, of which waited for: 2 -> 3; matrix products, arithmetic and copies ran while one was open for 1% -> 1% of each run, Pallas kernels for 14% -> 13%
where the time goes in v2:
time: 220 us; the launch traced here: 216 us
  blocking collectives  90.9 us (41%)
  Pallas kernels  59.8 us (27%)
  waiting for transfers between devices  22 us (10%)
  other arithmetic  17.9 us (8%)
  starting transfers between devices  17.1 us (8%)
  local copies, waits for them, and re-layouts  7.32 us (3%)
    all_to_all x1, blocking collectives, local(): got = lax.all_to_all(send, 'head', split_axis=0, concat_axis=0, tiled=True)  46.2 us
    all_to_all x1, blocking collectives, local(): back = lax.all_to_all(dx, 'head', split_axis=0, concat_axis=0, tiled=True)  44.7 us
    pallas_call x2, Pallas kernels, intra(): pl.pallas_call(partial(intra_kernel, head_dim), grid=(blocks, share), in_...  28.5 us
    pallas_call x1, Pallas kernels, local(): pl.pallas_call(partial(carry_kernel, head_dim), grid=(blocks, groups), in...  20.2 us
    all_to_all x2, waiting for transfers between devices, columns(): return lax.all_to_all(value, 'ctx', split_axis=0, concat_axis=0, tiled=True)  18.6 us
    all_to_all x2, starting transfers between devices, columns(): return lax.all_to_all(value, 'ctx', split_axis=0, concat_axis=0, tiled=True)  10.4 us
    pallas_call x1, Pallas kernels, local(): pl.pallas_call(partial(states_kernel, head_dim), grid=(groups, blocks), i...  9.98 us
    ppermute x2, starting transfers between devices, shifted(): return lax.ppermute(value, axis, pairs)  6.63 us
  transfers between devices with their start and end apart: 4, of which 3 were waited for; matrix products, arithmetic and copies ran while one was open for 1% of the time, Pallas kernels for 13%

profile of v2, /device:TPU:25, one launch (start us, length us, event | category | flops | bytes accessed | tf_op | source)
XLA Modules:
  0.0 216.0 jit_solution(11832494455406368848)
XLA Ops:
  0.6 0.0 copy-start.12
  0.6 1.0 slice.73
  1.6 3.7 %collective-permute-start = (bf16[3,8448]{1,0:T(4,128)(2,1)S(1)}, bf16[3,8448]{1,0:T(4,128)(2,1)S(1)}, u32[]{:S(2)}, u32[]{:S(2)}) collective-permute-start(bf16[3,8448]{1,0:T(4,128)(2,1)S(1)} %slice.73), channel_id=1, source_target_pairs={{0,1},{1,2},{2,3},{3,4},{4,5},{5,6},{6,7},{7,8},{8,9},{9,10},{10,1... | collective-permute-start | bytes 152072 | tf_op jit(solution)/shard_map/ppermute | solution.py:249
  5.3 1.6 slice_reduce_fusion.4
  6.9 0.0 copy-start.8
  6.9 0.0 copy-start.10
  6.9 0.0 collective-permute-done
  6.9 2.6 %maximum_convert_fusion = f32[195,8448]{1,0:T(8,128)S(1)} fusion(bf16[192,8448]{1,0:T(8,128)(2,1)} %param.7, bf16[3,8448]{1,0:T(4,128)(2,1)S(1)} %collective-permute-done), kind=kLoop, calls=%fused_computation.30 | loop fusion | flops 6589440 | bytes 9884160 | tf_op jit(solution)/shard_map/convert_element_type | solution.py:268
  9.5 0.0 copy-done.12
  9.5 5.6 %multiply_convert_fusion = (bf16[192,8448]{1,0:T(8,128)(2,1)S(1)}, f32[192,8448]{1,0:T(8,128)}) fusion(f32[195,8448]{1,0:T(8,128)S(1)} %maximum_convert_fusion, f32[8448]{0:T(1024)S(1)} %get-tuple-element.46, f32[8448]{0:T(1024)S(1)} %get-tuple-element.47, f32[8448]{0:T(1024)S(1)} %get-tuple-element.45, f32[8448]{0:T(1024)S(1)} %get-tuple-element.44, ...), kind=kLoop, calls=%fused_computation.27 | loop fusion | flops 21086208 | bytes 35853312 | tf_op jit(solution)/shard_map/convert_element_type | solution.py:273
  15.1 0.0 copy-done.8
  15.1 0.0 copy-done.10
  15.1 0.1 concatenate.32
  15.2 0.3 fusion.20
  15.5 0.0 copy-start
  15.5 0.0 copy-start.1
  15.5 2.6 %pad_maximum_fusion.1 = bf16[768,2304]{1,0:T(8,128)(2,1)S(1)} fusion(bf16[192,2304]{1,0:T(8,128)(2,1)S(1)} %concatenate.32, bf16[192,256]{1,0:T(8,128)(2,1)S(1)} %slice.99, bf16[192,2048]{1,0:T(8,128)(2,1)S(1)} %get-tuple-element.51, bf16[192,2048]{1,0:T(8,128)(2,1)S(1)} %get-tuple-element.52, bf16[192,2048]{1,0:T(8,128)(2,1)S(1)} %get-tuple-element.50), kind=kLoop, calls=%fused_computation.29 | loop fusion | flops 24772608 | bytes 6881280 | tf_op jit(solution)/shard_map/concatenate | solution.py:275
  18.1 46.2 %all_to_all.30 = bf16[4,192,2304]{2,1,0:T(8,128)(2,1)} all-to-all(bf16[4,192,2304]{2,1,0:T(8,128)(2,1)S(1)} %bitcast.29), channel_id=1, replica_groups=mesh['ctx'=8,'head'=4] {'head'}, dimensions={0} | all-to-all | bytes 7077888 | tf_op jit(solution)/shard_map/all_to_all | solution.py:282
  64.3 0.0 copy-start.13
  64.3 0.0 copy-done
  64.3 0.0 copy-done.1
  64.3 10.0 %states.1 = (f32[3,128,2048]{2,1,0:T(8,128)}, f32[3,128,2048]{2,1,0:T(8,128)}, f32[3,16,2048]{2,1,0:T(8,128)S(1)}, bf16[8,288,256]{2,1,0:T(8,128)(2,1)}) custom-call(bf16[768,2304]{1,0:T(8,128)(2,1)} %bitcast.19, bf16[768,2304]{1,0:T(8,128)(2,1)} %bitcast.20, bf16[768,2048]{1,0:T(8,128)(2,1)} %dy_ref.7, f32[32,768]{1,0:T(8,128)S(1)} %copy-done, ...), custom_call_target="tpu_custom_call" | custom-call | tf_op jit(solution)/shard_map/states/pallas_call | solution.py:304
  74.3 4.6 %all-to-all-start.1 = ((bf16[8,288,256]{2,1,0:T(8,128)(2,1)}), bf16[8,288,256]{2,1,0:T(8,128)(2,1)S(1)}, u32[]{:S(2)}, u32[]{:S(2)}) async-start(bf16[8,288,256]{2,1,0:T(8,128)(2,1)} %get-tuple-element.26), calls=%async_computation.1 | async-start | bytes 2359296 | tf_op jit(solution)/shard_map/all_to_all | solution.py:330
  78.9 0.0 copy-done.13
  78.9 0.1 broadcast_in_dim.11
  79.0 0.1 broadcast_in_dim.12
  79.1 14.2 %intra.2 = (bf16[768,2048]{1,0:T(8,128)(2,1)}, bf16[768,2048]{1,0:T(8,128)(2,1)}, f32[32,768]{1,0:T(8,128)S(1)}, f32[32,768]{1,0:T(8,128)S(1)}, f32[768,256]{1,0:T(8,128)S(1)}) custom-call(bf16[768,2304]{1,0:T(8,128)(2,1)} %bitcast.21, bf16[768,2304]{1,0:T(8,128)(2,1)} %bitcast.22, bf16[768,2048]{1,0:T(8,128)(2,1)} %dy_ref.7, f32[32,768]{1,0:T(8,128)S(1)} %copy-done, ...), custom_call_target="tpu_custom_call" | custom-call | flops 10000000000 | bytes 50000000 | tf_op jit(solution)/shard_map/intra/pallas_call | solution.py:350
  93.3 0.0 copy-start.2
  93.3 0.6 copy-done.2
  94.0 0.0 copy-start.4
  94.0 11.4 %all-to-all-done.1.in_ref = bf16[8,288,256]{2,1,0:T(8,128)(2,1)S(1)} async-done(((bf16[8,288,256]{2,1,0:T(8,128)(2,1)}), bf16[8,288,256]{2,1,0:T(8,128)(2,1)S(1)}, u32[]{:S(2)}, u32[]{:S(2)}) %all-to-all-start.1) | async-done | bytes 1179680 | tf_op jit(solution)/shard_map/all_to_all | solution.py:330
  105.4 1.2 chain.1
  106.6 5.8 %all-to-all-start.2 = ((bf16[8,256,256]{2,1,0:T(8,128)(2,1)}), bf16[8,256,256]{2,1,0:T(8,128)(2,1)S(1)}, u32[]{:S(2)}, u32[]{:S(2)}) async-start(bf16[8,256,256]{2,1,0:T(8,128)(2,1)} %chain.1), calls=%async_computation.2 | async-start | bytes 2097152 | tf_op jit(solution)/shard_map/all_to_all | solution.py:330
  112.4 0.0 copy-done.4
  112.4 0.0 copy-start.3
  112.5 0.9 copy-done.3
  113.3 0.0 copy-start.5
  113.3 0.9 copy-done.5
  114.2 14.2 %intra.3 = (bf16[768,2048]{1,0:T(8,128)(2,1)}, bf16[768,2048]{1,0:T(8,128)(2,1)}, f32[32,768]{1,0:T(8,128)S(1)}, f32[32,768]{1,0:T(8,128)S(1)}, f32[768,256]{1,0:T(8,128)S(1)}) custom-call(bf16[768,2304]{1,0:T(8,128)(2,1)} %bitcast.23, bf16[768,2304]{1,0:T(8,128)(2,1)} %bitcast.24, ...), custom_call_target="tpu_custom_call", output_to_operand_aliasing={{0}: (6, {}), {1}: (7, {}), {2}: (8, {}), {3}: (9, {})} | custom-call | flops 10000000000 | bytes 50000000 | tf_op jit(solution)/shard_map/intra/pallas_call | solution.py:350
  128.4 0.0 copy-start.6
  128.5 0.6 copy-done.6
  129.1 7.2 %all-to-all-done.2.enter_ref = bf16[8,256,256]{2,1,0:T(8,128)(2,1)S(1)} async-done(((bf16[8,256,256]{2,1,0:T(8,128)(2,1)}), bf16[8,256,256]{2,1,0:T(8,128)(2,1)S(1)}, u32[]{:S(2)}, u32[]{:S(2)}) %all-to-all-start.2) | async-done | bytes 1048608 | tf_op jit(solution)/shard_map/all_to_all | solution.py:330
  136.3 0.0 copy-start.7
  136.3 0.9 copy-done.7
  137.2 20.2 %carry.1 = (bf16[768,2048]{1,0:T(8,128)(2,1)}, bf16[768,2304]{1,0:T(8,128)(2,1)}, f32[32,768]{1,0:T(8,128)}, f32[32,768]{1,0:T(8,128)}) custom-call(bf16[768,2304]{1,0:T(8,128)(2,1)} %bitcast.25, bf16[768,2304]{1,0:T(8,128)(2,1)} %bitcast.26, bf16[768,2048]{1,0:T(8,128)(2,1)} %dy_ref.7, f32[32,768]{1,0:T(8,128)S(1)} %copy-done, f32[32,768]{1,0:T(8,128)S(1)} %copy-done.1, ...), custom_call_target="tpu_custom_call" | custom-call | tf_op jit(solution)/shard_map/carry/pallas_call | solution.py:390
  157.4 0.0 slice-start
  157.4 0.0 slice-start.1
  157.4 44.7 %all_to_all.31 = bf16[4,192,2304]{2,1,0:T(8,128)(2,1)S(1)} all-to-all(bf16[4,192,2304]{2,1,0:T(8,128)(2,1)} %bitcast.30), channel_id=1, replica_groups=mesh['ctx'=8,'head'=4] {'head'}, dimensions={0} | all-to-all | bytes 7077888 | tf_op jit(solution)/shard_map/all_to_all | solution.py:423
  202.1 0.1 slice_reduce_fusion
  202.2 0.1 fusion.18
  202.2 0.1 fusion.17
  202.3 0.1 fusion.16
  202.4 0.1 fusion.15
  202.4 0.0 slice-done
  202.5 0.0 slice-done.1
  202.5 0.0 copy-start.9
  202.5 0.0 copy-start.11
  202.5 2.4 %fusion.8 = f32[192,8448]{1,0:T(8,128)S(1)} fusion(bf16[192,8448]{1,0:T(8,128)(2,1)S(1)} %constant_dynamic-update-slice_fusion, f32[192,8448]{1,0:T(8,128)S(1)} %bitcast.28), kind=kLoop, calls=%fused_computation.15 | loop fusion | flops 16220160 | bytes 16220160 | tf_op jit(solution)/shard_map/transpose(jvp(jit(silu)))/add_any | solution.py:272
  204.9 2.9 %collective-permute-start.1 = (f32[3,8448]{1,0:T(4,128)S(1)}, f32[3,8448]{1,0:T(4,128)S(1)}, u32[]{:S(2)}, u32[]{:S(2)}) collective-permute-start(f32[3,8448]{1,0:T(4,128)S(1)} %slice.107), channel_id=1, source_target_pairs={{1,0},{2,1},{3,2},{4,3},{5,4},{6,5},{7,6},{8,7},{9,8},{10,9},{11,1... | collective-permute-start | bytes 304136 | tf_op jit(solution)/shard_map/ppermute | solution.py:249
  207.9 3.4 %collective-permute-done.1 = f32[3,8448]{1,0:T(4,128)S(1)} collective-permute-done((f32[3,8448]{1,0:T(4,128)S(1)}, f32[3,8448]{1,0:T(4,128)S(1)}, u32[]{:S(2)}, u32[]{:S(2)}) %collective-permute-start.1) | collective-permute-done | bytes 101408 | tf_op jit(solution)/shard_map/ppermute | solution.py:249
  211.3 0.0 copy-done.9
  211.3 0.0 copy-done.11
  211.3 4.7 %fusion.4 = bf16[192,8448]{1,0:T(8,128)(2,1)} fusion(f32[192,8448]{1,0:T(8,128)S(1)} %fusion.8, f32[3,8448]{1,0:T(4,128)S(1)} %collective-permute-done.1, f32[8448]{0:T(1024)S(1)} %copy-done.9, f32[8448]{0:T(1024)S(1)} %copy-done.11, f32[8448]{0:T(1024)S(1)} %get-tuple-element.45, f32[8448]{0:T(1024)S(1)} %get-tuple-element.44), kind=kLoop, calls=%fused_computation.11 | loop fusion | flops 17842176 | bytes 9968640 | tf_op jit(solution)/shard_map/convert_element_type | solution.py:434
  (5 shorter events, 0.0 us)
Async XLA Ops:
  0.6 8.9 %copy-start.12 = (f32[8448]{0:T(1024)S(1)}, f32[8448]{0:T(1024)}, u32[]{:S(2)}) copy-start(f32[8448]{0:T(1024)} %param.9) | copy-start | bytes 101380
  1.6 5.3 %collective-permute-start = (bf16[3,8448]{1,0:T(4,128)(2,1)S(1)}, bf16[3,8448]{1,0:T(4,128)(2,1)S(1)}, u32[]{:S(2)}, u32[]{:S(2)}) collective-permute-start(bf16[3,8448]{1,0:T(4,128)(2,1)S(1)} %slice.73), channel_id=1, source_target_pairs={{0,1},{1,2},{2,3},{3,4},{4,5},{5,6},{6,7},{7,8},{8,9},{9,10},{10,1... | collective-permute-start | bytes 152072 | tf_op jit(solution)/shard_map/ppermute | solution.py:249
  6.9 8.2 %copy-start.8 = (f32[8448]{0:T(1024)}, f32[8448]{0:T(1024)S(1)}, u32[]{:S(2)}) copy-start(f32[8448]{0:T(1024)S(1)} %get-tuple-element.46) | copy-start | bytes 101380
  6.9 8.2 %copy-start.10 = (f32[8448]{0:T(1024)}, f32[8448]{0:T(1024)S(1)}, u32[]{:S(2)}) copy-start(f32[8448]{0:T(1024)S(1)} %get-tuple-element.47) | copy-start | bytes 101380
  15.5 48.8 %copy-start = (f32[32,768]{1,0:T(8,128)S(1)}, f32[32,768]{1,0:T(8,128)}, u32[]{:S(2)}) copy-start(f32[32,768]{1,0:T(8,128)} %rate_ref.7) | copy-start | bytes 294916
  15.5 48.8 %copy-start.1 = (f32[32,768]{1,0:T(8,128)S(1)}, f32[32,768]{1,0:T(8,128)}, u32[]{:S(2)}) copy-start(f32[32,768]{1,0:T(8,128)} %step_ref.7) | copy-start | bytes 294916
  64.3 14.6 %copy-start.13 = (f32[32]{0:T(128)S(1)}, f32[32]{0:T(128)}, u32[]{:S(2)}) copy-start(f32[32]{0:T(128)} %param.12) | copy-start | bytes 388
  74.3 31.1 %all-to-all-start.1 = ((bf16[8,288,256]{2,1,0:T(8,128)(2,1)}), bf16[8,288,256]{2,1,0:T(8,128)(2,1)S(1)}, u32[]{:S(2)}, u32[]{:S(2)}) async-start(bf16[8,288,256]{2,1,0:T(8,128)(2,1)} %get-tuple-element.26), calls=%async_computation.1 | async-start | bytes 2359296 | tf_op jit(solution)/shard_map/all_to_all | solution.py:330
  93.3 0.6 copy-start.2
  94.0 18.5 %copy-start.4 = (f32[32,768]{1,0:T(8,128)}, f32[32,768]{1,0:T(8,128)S(1)}, u32[]{:S(2)}) copy-start(f32[32,768]{1,0:T(8,128)S(1)} %get-tuple-element.29.refs_3_) | copy-start | bytes 294916
  106.6 29.7 %all-to-all-start.2 = ((bf16[8,256,256]{2,1,0:T(8,128)(2,1)}), bf16[8,256,256]{2,1,0:T(8,128)(2,1)S(1)}, u32[]{:S(2)}, u32[]{:S(2)}) async-start(bf16[8,256,256]{2,1,0:T(8,128)(2,1)} %chain.1), calls=%async_computation.2 | async-start | bytes 2097152 | tf_op jit(solution)/shard_map/all_to_all | solution.py:330
  112.4 0.9 copy-start.3
  113.3 0.9 copy-start.5
  128.4 0.6 copy-start.6
  136.3 0.9 copy-start.7
  157.4 45.1 %slice-start = ((s8[6488064]{0:T(1024)(128)(4,1)}), s8[4194304]{0:T(1024)(128)(4,1)S(1)}, s32[]{:S(2)}) async-start(s8[6488064]{0:T(1024)(128)(4,1)} %bitcast.27), calls=%async_computation.4 | async-start | bytes 8388608
  157.4 45.1 %slice-start.1 = ((s8[6488064]{0:T(1024)(128)(4,1)}), s8[2293760]{0:T(1024)(128)(4,1)S(1)}, s32[]{:S(2)}) async-start(s8[6488064]{0:T(1024)(128)(4,1)} %bitcast.27), calls=%async_computation.5 | async-start | bytes 4587520
  202.5 8.8 %copy-start.9 = (f32[8448]{0:T(1024)S(1)}, f32[8448]{0:T(1024)}, u32[]{:S(2)}) copy-start(f32[8448]{0:T(1024)} %copy-done.8) | copy-start | bytes 101380
  202.5 8.8 %copy-start.11 = (f32[8448]{0:T(1024)S(1)}, f32[8448]{0:T(1024)}, u32[]{:S(2)}) copy-start(f32[8448]{0:T(1024)} %copy-done.10) | copy-start | bytes 101380
  204.9 6.3 %collective-permute-start.1 = (f32[3,8448]{1,0:T(4,128)S(1)}, f32[3,8448]{1,0:T(4,128)S(1)}, u32[]{:S(2)}, u32[]{:S(2)}) collective-permute-start(f32[3,8448]{1,0:T(4,128)S(1)} %slice.107), channel_id=1, source_target_pairs={{1,0},{2,1},{3,2},{4,3},{5,4},{6,5},{7,6},{8,7},{9,8},{10,9},{11,1... | collective-permute-start | bytes 304136 | tf_op jit(solution)/shard_map/ppermute | solution.py:249
